TPU v7x, 32 devices: a whole 2x2x4 slice. The times are simulated.
32 devices in a mesh: dp: 8 (over z, y), seq: 4 (over x, core).
Axes of the slice: x: 2, y: 2, z: 4, core: 2. Of those that a mesh axis runs over, the one named last changes fastest.
Arguments:
- inputs: bfloat16 [8, 512, 4096], P('dp', 'seq'), may hold values from -6 to 6
- raw_step: bfloat16 [8, 512, 64], P('dp', 'seq'), may hold values from -5 to 5
- write_keys: bfloat16 [8, 512, 128], P('dp', 'seq'), may hold values from -0.5 to 0.5
- read_keys: bfloat16 [8, 512, 128], P('dp', 'seq'), may hold values from -0.5 to 0.5
- grad_out: bfloat16 [8, 512, 4096], P('dp', 'seq'), may hold values from -6 to 6
- decay_log: float32 [64], P('seq'), as said below
- skip_gain: float32 [64], P('seq'), may hold values from 0.5 to 1.5
- step_bias: float32 [64], P('seq'), may hold values from -1 to 1
Outputs:
- grad_x: bfloat16 [8, 512, 4096], P('dp', 'seq')
- grad_step: bfloat16 [8, 512, 64], P('dp', 'seq')
- grad_write: bfloat16 [8, 512, 128], P('dp', 'seq')
- grad_read: bfloat16 [8, 512, 128], P('dp', 'seq')
- grad_params: float32 [3, 64], P(None, 'seq')
Inputs may be any that keep to these rules, and one draw needn't show every extreme that they name: exp(decay_log) lies between 0.2 / 512 and 1 / 20.
All inputs are finite; a program needn't handle non-finite values.
Results may differ from a plain program's by a relative error of at most 0.002.
Values may be sent and summed in bfloat16 or wider, within the bound.
A program may use at most 128 MiB of HBM per device.

v0:
```python
import functools

import jax
import jax.numpy as jnp
from jax import lax
from jax.experimental import pallas as pl
from jax.experimental.pallas import tpu as pltpu
from jax.sharding import PartitionSpec as P

LANES = 128
ROWS = 16
LOG2E = 1.4426950408889634
bf16 = jnp.bfloat16
f32 = jnp.float32


def iota(shape, dim):
    return lax.broadcasted_iota(jnp.int32, shape, dim)


def dot_nt(a, b):
    return lax.dot_general(a, b, (((1,), (1,)), ((), ())), preferred_element_type=f32)


def dot_nn(a, b):
    return jnp.dot(a, b, preferred_element_type=f32)


def split_two(v):
    hi = v.astype(bf16)
    return hi, (v - hi.astype(f32)).astype(bf16)


def scan_lanes(v, reverse):
    rows, length = v.shape
    width = min(256, length)
    r, c = iota((width, width), 0), iota((width, width), 1)
    keep = (r >= c) if reverse else (r <= c)
    ones = jnp.where(keep, 1.0, 0.0).astype(bf16)
    one = v.astype(bf16)
    rest = v - one.astype(f32)
    two = rest.astype(bf16)
    three = (rest - two.astype(f32)).astype(bf16)
    stacked = jnp.concatenate([one, two, three], axis=0)
    spots = list(range(0, length, width))
    carry = jnp.zeros((rows, 1), f32)
    out = {}
    for start in reversed(spots) if reverse else spots:
        part = dot_nn(stacked[:, start : start + width], ones)
        part = part[:rows] + (part[rows : 2 * rows] + part[2 * rows :]) + carry
        out[start] = part
        carry = part[:, :1] if reverse else part[:, width - 1 :]
    return jnp.concatenate([out[s] for s in spots], axis=1)


def prepare(raw, decay, bias, wide, small, arow, acol, dts, sig, rate, heads):
    length = raw.shape[0]
    wide[...] = jnp.zeros_like(wide)
    wide[:, :heads] = raw[...].astype(f32) + bias[...]
    z = wide[...].T[:heads]
    small[...] = jnp.zeros_like(small)
    small[0:1, :heads] = jnp.exp(decay[...])
    rate_col = jnp.broadcast_to(small[0:1, :], (LANES, LANES)).T[:heads]
    rate[...] = rate_col
    dt = jnp.maximum(z, 0.0) + jnp.log1p(jnp.exp(-jnp.abs(z)))
    dts[...] = dt
    sig[...] = 1.0 / (1.0 + jnp.exp(-z))
    a = scan_lanes(dt * (rate_col[:, :1] * -LOG2E), False)
    for h in range(heads):
        arow[h] = jnp.broadcast_to(a[h : h + 1, :], (8, length))
    below = a - jnp.log(dt) * LOG2E
    column = jnp.concatenate([below, jnp.zeros((LANES - heads, length), f32)], axis=0).T
    for h in range(heads):
        acol[h] = jnp.broadcast_to(column[:, h : h + 1], (length, LANES))


def tile(pair, s0, t0, width, diagonal, x, g, scr):
    w, m, vacc = scr["w"], scr["m"], scr["vacc"]
    lanes = pl.ds(pl.multiple_of(pair * LANES, LANES), LANES)
    srows, trows = pl.ds(s0, LANES), pl.ds(t0, width)
    xs = x[srows, lanes]
    gs = g[trows, lanes]
    low = iota((width, LANES), 1) < LANES // 2
    zero = jnp.zeros_like(gs)
    parts = (jnp.where(low, gs, zero), jnp.where(low, zero, gs))
    for k in range(2):
        w[k, :, :width] = dot_nt(xs, parts[k])
    lane = iota((ROWS, LANES), 1)
    at = [scr["arow"][2 * pair + k, :, trows] for k in range(2)]
    at = [jnp.concatenate([v] * (ROWS // 8), axis=0) for v in at]
    sums = [None, None]
    for c in range(LANES // ROWS):
        rows = pl.ds(s0 + c * ROWS, ROWS)
        here = slice(c * ROWS, (c + 1) * ROWS)
        s_tile = scr["score"][rows, trows]
        q = scr["q"][rows, trows]
        col = scr["col"][rows, :]
        for k in range(2):
            ac = scr["acol"][2 * pair + k, rows, :]
            gap = at[k] - jnp.concatenate([ac] * (width // LANES), axis=1)
            if diagonal:
                keep = iota((ROWS, width), 1) >= iota((ROWS, width), 0) + c * ROWS
                gap = jnp.where(keep, gap, -jnp.inf)
            lp = jnp.exp2(gap)
            wk = w[k, here, :width]
            q = q + lp * wk
            mk = lp * s_tile
            hi, lo = split_two(mk)
            m[2 * k, here, :width] = hi
            m[2 * k + 1, here, :width] = lo
            zk = mk * wk
            part = zk[:8] + zk[8:]
            sums[k] = part if sums[k] is None else sums[k] + part
            across = zk[:, :LANES]
            for j in range(1, width // LANES):
                across = across + zk[:, j * LANES : (j + 1) * LANES]
            total = jnp.sum(across, axis=1, keepdims=True)
            col = col + jnp.where(lane == 2 * pair + k, total, 0.0)
        scr["q"][rows, trows] = q
        scr["col"][rows, :] = col
    for k in range(2):
        scr["racc"][k, :, trows] += sums[k]
    v = None
    for k in range(2):
        for j in range(2):
            term = dot_nn(m[2 * k + j, :, :width], parts[k])
            v = term if v is None else v + term
    return v


def one_pair(pair, x, g, skip, dx, scr, length):
    lanes = pl.ds(pl.multiple_of(pair * LANES, LANES), LANES)
    scr["racc"][...] = jnp.zeros_like(scr["racc"])
    low = iota((1, LANES), 1) < LANES // 2
    gain = jnp.where(low, skip[2 * pair], skip[2 * pair + 1])
    blocks = length // LANES

    def finish(s0, v):
        rows = pl.ds(s0, LANES)
        gs = g[rows, lanes].astype(f32)
        dx[rows, lanes] = (v + gain * gs).astype(bf16)
        scr["direct"][...] += jnp.sum(
            (x[rows, lanes].astype(f32) * gs).reshape(LANES // 8, 8, LANES), axis=0
        )

    scr["direct"][...] = jnp.zeros_like(scr["direct"])
    if blocks <= 4:
        for i in range(blocks):
            s0 = i * LANES
            finish(s0, tile(pair, s0, s0, length - s0, True, x, g, scr))
    else:

        def block(i, _):
            s0 = pl.multiple_of(i * LANES, LANES)
            scr["vacc"][...] = tile(pair, s0, s0, LANES, True, x, g, scr)

            def right(j, _):
                t0 = pl.multiple_of(j * LANES, LANES)
                scr["vacc"][...] += tile(pair, s0, t0, LANES, False, x, g, scr)
                return 0

            lax.fori_loop(i + 1, blocks, right, 0)
            finish(s0, scr["vacc"][...])
            return 0

        lax.fori_loop(0, blocks, block, 0)
    direct = jnp.sum(scr["direct"][...], axis=0, keepdims=True)
    for k in range(2):
        scr["row"][pl.ds(2 * pair + k, 1), :] = jnp.sum(scr["racc"][k], axis=0, keepdims=True)
        mine = jnp.where(low, direct, 0.0) if k == 0 else jnp.where(low, 0.0, direct)
        scr["gain"][pl.ds(2 * pair + k, 1), :] = jnp.broadcast_to(
            jnp.sum(mine, axis=1, keepdims=True), (1, LANES)
        )


def scores(bk, ck, scr, length):
    blocks = length // LANES
    for i in range(blocks):
        s0 = i * LANES
        scr["score"][s0 : s0 + LANES, s0:] = dot_nt(bk[s0 : s0 + LANES, :], ck[s0:, :])
        scr["q"][s0 : s0 + LANES, s0:] = jnp.zeros((LANES, length - s0), f32)


def step_grads(scr, heads, length):
    col = scr["col"][...].T[:heads]
    dl = scan_lanes(scr["row"][...] - col, True)
    rate = scr["rate"][:, :1]
    dt = scr["dts"][...]
    ddt = col / dt - rate * dl
    draw = ddt * scr["sig"][...]
    pad = jnp.zeros((LANES - heads, length), f32)
    step = jnp.concatenate([draw, pad], axis=0).T
    decay = -rate * jnp.sum(dl * dt, axis=1, keepdims=True)
    shift = jnp.sum(draw, axis=1, keepdims=True)
    lane = iota((heads, LANES), 1)
    params = jnp.where(lane == 0, decay, jnp.where(lane == 1, scr["gain"][...], shift))
    params = jnp.concatenate([params, jnp.zeros((LANES - heads, LANES), f32)], axis=0).T
    return step[:, :heads], params[:3, :heads]


def key_grads(bk, ck, scr, length, write):
    blocks = length // LANES
    bt = bk[...].astype(f32).T.astype(bf16)
    for i in range(blocks):
        here = slice(i * LANES, (i + 1) * LANES)
        hi, lo = split_two(scr["q"][here, i * LANES :])
        db = dot_nn(hi, ck[i * LANES :, :]) + dot_nn(lo, ck[i * LANES :, :])
        upto = (i + 1) * LANES
        hi, lo = split_two(scr["q"][:upto, here])
        dc = dot_nn(bt[:, :upto], hi) + dot_nn(bt[:, :upto], lo)
        write(i, db, dc.T)


def scratch(heads, length):
    width = length if length <= 4 * LANES else LANES
    return {
        "wide": pltpu.VMEM((length, LANES), f32),
        "small": pltpu.VMEM((8, LANES), f32),
        "arow": pltpu.VMEM((heads, 8, length), f32),
        "acol": pltpu.VMEM((heads, length, LANES), f32),
        "dts": pltpu.VMEM((heads, length), f32),
        "sig": pltpu.VMEM((heads, length), f32),
        "rate": pltpu.VMEM((heads, LANES), f32),
        "score": pltpu.VMEM((length, length), f32),
        "q": pltpu.VMEM((length, length), f32),
        "col": pltpu.VMEM((length, LANES), f32),
        "row": pltpu.VMEM((heads, length), f32),
        "gain": pltpu.VMEM((heads, LANES), f32),
        "racc": pltpu.VMEM((2, 8, length), f32),
        "direct": pltpu.VMEM((8, LANES), f32),
        "vacc": pltpu.VMEM((LANES, LANES), f32),
        "w": pltpu.VMEM((2, LANES, width), f32),
        "m": pltpu.VMEM((4, LANES, width), bf16),
    }


def kernel(names, heads, length, x, raw, bk, ck, g, decay, skip, bias, dx, step, dkeys, par, *rest):
    scr = dict(zip(names, rest))
    prepare(
        raw, decay, bias, scr["wide"], scr["small"], scr["arow"], scr["acol"],
        scr["dts"], scr["sig"], scr["rate"], heads,
    )
    scores(bk, ck, scr, length)
    scr["col"][...] = jnp.zeros_like(scr["col"])

    def body(pair, _):
        one_pair(pair, x, g, skip, dx, scr, length)
        return 0

    lax.fori_loop(0, heads // 2, body, 0)
    step_out, par_out = step_grads(scr, heads, length)
    step[...] = step_out.astype(bf16)
    par[...] = par_out

    def write(i, db, dc):
        rows = slice(i * LANES, (i + 1) * LANES)
        dkeys[rows, :LANES] = db
        dkeys[rows, LANES:] = dc

    key_grads(bk, ck, scr, length, write)


def backward(x, raw, bk, ck, g, decay, skip, bias):
    length, heads = raw.shape
    space = scratch(heads, length)
    vmem = pl.BlockSpec(memory_space=pltpu.VMEM)
    smem = pl.BlockSpec(memory_space=pltpu.SMEM)
    return pl.pallas_call(
        functools.partial(kernel, tuple(space), heads, length),
        out_shape=(
            jax.ShapeDtypeStruct(x.shape, bf16),
            jax.ShapeDtypeStruct(raw.shape, bf16),
            jax.ShapeDtypeStruct((length, 2 * LANES), f32),
            jax.ShapeDtypeStruct((3, heads), f32),
        ),
        in_specs=[vmem, vmem, vmem, vmem, vmem, vmem, smem, vmem],
        out_specs=(vmem, vmem, vmem, vmem),
        scratch_shapes=list(space.values()),
        compiler_params=pltpu.CompilerParams(vmem_limit_bytes=60 * 1024 * 1024),
    )(x, raw, bk, ck, g, decay.reshape(1, heads), skip, bias.reshape(1, heads))


def shards(inputs, raw_step, write_keys, read_keys, grad_out, decay_log, skip_gain, step_bias):
    replicas = lax.axis_size("dp")
    swap = functools.partial(lax.all_to_all, axis_name="seq", split_axis=1, concat_axis=0, tiled=True)
    x, g, raw = swap(inputs[0]), swap(grad_out[0]), swap(raw_step[0])
    keys = lax.all_gather(jnp.concatenate([write_keys[0], read_keys[0]], axis=1), "seq", axis=0, tiled=True)
    dx, step, dkeys, par = backward(
        x, raw, keys[:, :LANES], keys[:, LANES:], g, decay_log, skip_gain, step_bias
    )
    back = functools.partial(lax.all_to_all, axis_name="seq", split_axis=0, concat_axis=1, tiled=True)
    grad_x, grad_step = back(dx), back(step)
    summed = lax.psum_scatter(dkeys, "seq", scatter_dimension=0, tiled=True).astype(bf16)
    total = lax.psum(par, "dp") / replicas
    return (
        grad_x[None], grad_step[None], summed[None, :, :LANES], summed[None, :, LANES:], total,
    )


def solution(mesh):
    rows = P("dp", "seq", None)
    return jax.shard_map(
        shards,
        mesh=mesh,
        in_specs=(rows,) * 5 + (P("seq"),) * 3,
        out_specs=(rows,) * 4 + (P(None, "seq"),),
        check_vma=False,
    )
```

profile of v0, /device:TPU:0, one launch (start us, length us, event | category | flops | bytes accessed | tf_op | source)
XLA Modules:
  0.0 114.9 jit_solution(16011296826704227194)
XLA Ops:
  7.2 4.2 %all-to-all-start.1 = ((bf16[128,4,16]{0,2,1:T(8,128)(2,1)}), bf16[128,4,16]{0,2,1:T(8,128)(2,1)S(1)}, u32[]{:S(2)}, u32[]{:S(2)}) async-start(bf16[128,4,16]{0,2,1:T(8,128)(2,1)} %bitcast.33), calls=%async_computation.1 | async-start | bytes 32768 | tf_op jit(solution)/shard_map/all_to_all | solution.py:286
  11.4 1.8 %all_to_all.66 = bf16[128,4,1024]{2,1,0:T(4,128)(2,1)S(1)} reshape(bf16[1,128,4096]{2,1,0:T(8,128)(2,1)} %param.8) | data formatting | bytes 2097152 | tf_op jit(solution)/shard_map/all_to_all | solution.py:286
  13.2 1.3 %copy.18 = bf16[128,4,1024]{2,0,1:T(8,128)(2,1)} copy(bf16[128,4,1024]{2,1,0:T(4,128)(2,1)S(1)} %all_to_all.66) | data formatting | bytes 2097152 | tf_op jit(solution)/shard_map/all_to_all | solution.py:286
  14.5 0.0 copy-start.2
  14.5 0.7 all-to-all-done.1
  15.2 3.5 %all-to-all-start = ((bf16[128,4,1024]{2,0,1:T(8,128)(2,1)}), bf16[128,4,1024]{2,0,1:T(8,128)(2,1)S(1)}, u32[]{:S(2)}, u32[]{:S(2)}) async-start(bf16[128,4,1024]{2,0,1:T(8,128)(2,1)} %copy.18), calls=%async_computation | async-start | bytes 2097152 | tf_op jit(solution)/shard_map/all_to_all | solution.py:286
  18.8 0.0 copy-done.2
  18.8 0.8 all_to_all.74
  19.6 1.3 %copy.20 = bf16[128,4,1024]{2,0,1:T(8,128)(2,1)} copy(bf16[128,4,1024]{2,1,0:T(4,128)(2,1)S(1)} %all_to_all.74) | data formatting | bytes 2097152 | tf_op jit(solution)/shard_map/all_to_all | solution.py:286
  20.9 0.0 copy-start.4
  20.9 0.0 copy-start.5
  20.9 12.3 %all-to-all-done = bf16[128,4,1024]{2,0,1:T(8,128)(2,1)S(1)} async-done(((bf16[128,4,1024]{2,0,1:T(8,128)(2,1)}), bf16[128,4,1024]{2,0,1:T(8,128)(2,1)S(1)}, u32[]{:S(2)}, u32[]{:S(2)}) %all-to-all-start) | async-done | bytes 1048608 | tf_op jit(solution)/shard_map/all_to_all | solution.py:286
  33.2 0.0 copy-start
  33.2 3.5 %all-to-all-start.2 = ((bf16[128,4,1024]{2,0,1:T(8,128)(2,1)}), bf16[128,4,1024]{2,0,1:T(8,128)(2,1)S(1)}, u32[]{:S(2)}, u32[]{:S(2)}) async-start(bf16[128,4,1024]{2,0,1:T(8,128)(2,1)} %copy.20), calls=%async_computation.2 | async-start | bytes 2097152 | tf_op jit(solution)/shard_map/all_to_all | solution.py:286
  36.7 0.0 reduce-scatter.2.cloned.1.call-start
  36.8 0.0 copy-done
  36.8 0.0 copy-done.4
  36.8 0.0 copy-done.5
  36.8 16.6 %all_gather.3 = bf16[512,256]{1,0:T(8,128)(2,1)S(1)} all-gather(bf16[128,256]{1,0:T(8,128)(2,1)S(1)} %pad_maximum_fusion), channel_id=1, replica_groups=mesh['dp'=8,'seq'=4] {'seq'}, dimensions={0}, use_global_device_ids=true | all-gather | bytes 327680 | tf_op jit(solution)/shard_map/all_gather | solution.py:287
  53.4 0.7 fusion
  54.1 0.8 copy.19
  54.9 0.0 all-to-all-done.2
  54.9 0.0 copy-start.1
  54.9 1.0 copy-done.1
  55.9 14.0 %shard_map.119 = (bf16[512,1024]{1,0:T(8,128)(2,1)}, bf16[512,16]{1,0:T(8,128)(2,1)}, f32[512,256]{1,0:T(8,128)}, f32[3,16]{1,0:T(4,128)}) custom-call(bf16[512,1024]{1,0:T(8,128)(2,1)} %bitcast.23, bf16[512,16]{1,0:T(8,128)(2,1)} %bitcast.27, bf16[512,128]{1,0:T(8,128)(2,1)} %get-tuple-element.14.bk, bf16[512,128]{1,0:T(8,128)(2,1)} %get-tuple-element.13.ck, ...), custom_call_target="tpu_custom_call" | custom-call | tf_op jit(solution)/shard_map/pallas_call | solution.py:268
  69.9 0.0 copy-start.3
  69.9 0.0 reduce-scatter.2.cloned.1.call-update
  69.9 0.9 copy-done.3
  70.8 0.1 copy.22
  70.8 6.2 %all_to_all.89 = bf16[4,128,16]{1,2,0:T(8,128)(2,1)S(1)} all-to-all(bf16[4,128,16]{1,2,0:T(8,128)(2,1)S(1)} %copy.22), channel_id=1, replica_groups=mesh['dp'=8,'seq'=4] {'seq'}, dimensions={0} | all-to-all | bytes 32768 | tf_op jit(solution)/shard_map/all_to_all | solution.py:292
  77.1 0.0 copy-start.6
  77.1 3.7 %all-to-all-start.3 = ((bf16[4,128,1024]{2,1,0:T(8,128)(2,1)}), bf16[4,128,1024]{2,1,0:T(8,128)(2,1)S(1)}, u32[]{:S(2)}, u32[]{:S(2)}) async-start(bf16[4,128,1024]{2,1,0:T(8,128)(2,1)} %bitcast.26), calls=%async_computation.3 | async-start | bytes 2097152 | tf_op jit(solution)/shard_map/all_to_all | solution.py:292
  80.7 0.0 copy-done.6
  80.7 22.1 %psum.7 = f32[3,16]{1,0:T(4,128)S(1)} all-reduce(f32[3,16]{1,0:T(4,128)S(1)} %copy-done.6), channel_id=1, replica_groups=mesh['dp'=8,'seq'=4] {'dp'}, use_global_device_ids=true, to_apply=%region_1.0 | all-reduce | flops 48 | bytes 384 | tf_op jit(solution)/shard_map/psum | solution.py:294
  102.9 0.6 broadcast_multiply_fusion
  103.5 0.0 all-to-all-done.3
  103.5 0.8 copy.21
  104.3 1.6 %broadcast_in_dim.12 = bf16[1,128,4096]{2,1,0:T(8,128)(2,1)} reshape(bf16[128,4,1024]{2,1,0:T(4,128)(2,1)S(1)} %copy.21) | data formatting | bytes 2097152 | tf_op jit(solution)/shard_map/broadcast_in_dim | solution.py:296
  105.9 0.0 reduce-scatter.2.cloned.1.call-done
  105.9 0.9 convert_element_type.3
  106.8 0.6 slice_bitcast_fusion
  107.4 0.6 copy.24
  (1 shorter events, 0.0 us)
Async XLA Ops:
  7.2 8.1 %all-to-all-start.1 = ((bf16[128,4,16]{0,2,1:T(8,128)(2,1)}), bf16[128,4,16]{0,2,1:T(8,128)(2,1)S(1)}, u32[]{:S(2)}, u32[]{:S(2)}) async-start(bf16[128,4,16]{0,2,1:T(8,128)(2,1)} %bitcast.33), calls=%async_computation.1 | async-start | bytes 32768 | tf_op jit(solution)/shard_map/all_to_all | solution.py:286
  14.5 4.2 %copy-start.2 = (bf16[1,128,4096]{2,1,0:T(8,128)(2,1)S(1)}, bf16[1,128,4096]{2,1,0:T(8,128)(2,1)}, u32[]{:S(2)}) copy-start(bf16[1,128,4096]{2,1,0:T(8,128)(2,1)} %param.12) | copy-start | bytes 3145732
  15.2 18.0 %all-to-all-start = ((bf16[128,4,1024]{2,0,1:T(8,128)(2,1)}), bf16[128,4,1024]{2,0,1:T(8,128)(2,1)S(1)}, u32[]{:S(2)}, u32[]{:S(2)}) async-start(bf16[128,4,1024]{2,0,1:T(8,128)(2,1)} %copy.18), calls=%async_computation | async-start | bytes 2097152 | tf_op jit(solution)/shard_map/all_to_all | solution.py:286
  20.9 15.9 %copy-start.4 = (bf16[1,128,128]{2,1,0:T(8,128)(2,1)S(1)}, bf16[1,128,128]{2,1,0:T(8,128)(2,1)}, u32[]{:S(2)}) copy-start(bf16[1,128,128]{2,1,0:T(8,128)(2,1)} %param.11) | copy-start | bytes 98308
  20.9 15.9 %copy-start.5 = (bf16[1,128,128]{2,1,0:T(8,128)(2,1)S(1)}, bf16[1,128,128]{2,1,0:T(8,128)(2,1)}, u32[]{:S(2)}) copy-start(bf16[1,128,128]{2,1,0:T(8,128)(2,1)} %param.10) | copy-start | bytes 98308
  33.2 3.6 %copy-start = (bf16[128,4,1024]{2,0,1:T(8,128)(2,1)}, bf16[128,4,1024]{2,0,1:T(8,128)(2,1)S(1)}, u32[]{:S(2)}) copy-start(bf16[128,4,1024]{2,0,1:T(8,128)(2,1)S(1)} %all-to-all-done) | copy-start | bytes 3145732
  33.2 21.7 %all-to-all-start.2 = ((bf16[128,4,1024]{2,0,1:T(8,128)(2,1)}), bf16[128,4,1024]{2,0,1:T(8,128)(2,1)S(1)}, u32[]{:S(2)}, u32[]{:S(2)}) async-start(bf16[128,4,1024]{2,0,1:T(8,128)(2,1)} %copy.20), calls=%async_computation.2 | async-start | bytes 2097152 | tf_op jit(solution)/shard_map/all_to_all | solution.py:286
  36.7 69.1 %reduce-scatter.2.cloned.1.call-start = ((), (), s32[]{:S(2)}) async-start(), calls=%async_computation.6 | async-start | bytes 655360 | tf_op jit(solution)/shard_map/reduce_scatter | solution.py:293
  54.9 1.0 copy-start.1
  69.9 0.9 copy-start.3
  77.1 3.7 %copy-start.6 = (f32[3,16]{1,0:T(4,128)S(1)}, f32[3,16]{1,0:T(4,128)}, u32[]{:S(2)}) copy-start(f32[3,16]{1,0:T(4,128)} %get-tuple-element.12) | copy-start | bytes 580
  77.1 26.4 %all-to-all-start.3 = ((bf16[4,128,1024]{2,1,0:T(8,128)(2,1)}), bf16[4,128,1024]{2,1,0:T(8,128)(2,1)S(1)}, u32[]{:S(2)}, u32[]{:S(2)}) async-start(bf16[4,128,1024]{2,1,0:T(8,128)(2,1)} %bitcast.26), calls=%async_computation.3 | async-start | bytes 2097152 | tf_op jit(solution)/shard_map/all_to_all | solution.py:292
Sparse Core Ops, SparseCore 0:
  70.0 25.4 reduce-scatter.1
where the time goes:
time: 115 us
  blocking collectives  44.9 us (39%)
  starting transfers between devices  14.9 us (13%)
  between operations  14.1 us (12%)
  Pallas kernels  14 us (12%)
  waiting for transfers between devices  13.1 us (11%)
  local copies, waits for them, and re-layouts  12.3 us (11%)
  other arithmetic  1.51 us (1%)
    psum x1, blocking collectives, shards(): total = lax.psum(par, 'dp') / replicas  22.1 us
    all_gather x1, blocking collectives, shards(): lax.all_gather(jnp.concatenate([write_keys[0], read_keys[0]], axis=1), 's...  16.6 us
    pallas_call x1, Pallas kernels, backward(): pl.pallas_call(functools.partial(kernel, tuple(space), heads, length), ou...  14 us
    all_to_all x3, waiting for transfers between devices, shards(): x, g, raw = (swap(inputs[0]), swap(grad_out[0]), swap(raw_step[0]))  13 us
    all_to_all x3, starting transfers between devices, shards(): x, g, raw = (swap(inputs[0]), swap(grad_out[0]), swap(raw_step[0]))  11.3 us
    all_to_all x1, blocking collectives, shards(): grad_x, grad_step = (back(dx), back(step))  6.21 us
    all_to_all x5, local copies, waits for them, and re-layouts, shards(): x, g, raw = (swap(inputs[0]), swap(grad_out[0]), swap(raw_step[0]))  5.98 us
    all_to_all x1, starting transfers between devices, shards(): grad_x, grad_step = (back(dx), back(step))  3.65 us
  transfers between devices with their start and end apart: 5, of which 2 were waited for; matrix products, arithmetic and copies ran while one was open for 6% of the time, Pallas kernels for 0%

commit v1 on v0

--- a/solution.py
+++ b/solution.py
@@ -53,12 +53,13 @@
     return jnp.concatenate([out[s] for s in spots], axis=1)
 
 
-def prepare(raw, decay, bias, wide, small, arow, acol, dts, sig, rate, heads):
-    length = raw.shape[0]
-    wide[...] = jnp.zeros_like(wide)
-    wide[:, :heads] = raw[...].astype(f32) + bias[...]
+def prepare(raw, offset, decay, bias, wide, small, arow, acol, dts, sig, rate, heads):
+    length, total = raw.shape
+    pick = jnp.where(iota((total, LANES), 0) == iota((total, LANES), 1) + offset, 1.0, 0.0)
+    small[...] = jnp.zeros_like(small)
+    small[1:2, :heads] = bias[...]
+    wide[...] = dot_nn(raw[...], pick.astype(bf16)) + small[1:2, :]
     z = wide[...].T[:heads]
-    small[...] = jnp.zeros_like(small)
     small[0:1, :heads] = jnp.exp(decay[...])
     rate_col = jnp.broadcast_to(small[0:1, :], (LANES, LANES)).T[:heads]
     rate[...] = rate_col
@@ -195,7 +196,7 @@
     lane = iota((heads, LANES), 1)
     params = jnp.where(lane == 0, decay, jnp.where(lane == 1, scr["gain"][...], shift))
     params = jnp.concatenate([params, jnp.zeros((LANES - heads, LANES), f32)], axis=0).T
-    return step[:, :heads], params[:3, :heads]
+    return step, params[:8]
 
 
 def key_grads(bk, ck, scr, length, write):
@@ -234,73 +235,254 @@
     }
 
 
-def kernel(names, heads, length, x, raw, bk, ck, g, decay, skip, bias, dx, step, dkeys, par, *rest):
+def kernel(names, n, replicas, x_hbm, raw, wk, rk, g_hbm, decay, skip, bias, dx_out, step, dwrite, dread, par, *rest):
     scr = dict(zip(names, rest))
+    rows = x_hbm.shape[0]
+    length = rows * n
+    heads = decay.shape[1]
+    pairs = heads // 2
+    span = pairs * LANES
+    me, dp = lax.axis_index("seq"), lax.axis_index("dp")
+    x, g, dx, bk, ck, raws = (scr[k] for k in ("x", "g", "dx", "bk", "ck", "raws"))
+    mine = pl.ds(pl.multiple_of(me * rows, rows), rows)
+    left = pl.ds(pl.multiple_of(me * span, span), span)
+
+    def seq(k):
+        return lax.rem(me + k, n)
+
+    def replica(k):
+        return lax.rem(dp + k, replicas)
+
+    def send(src, dst, out_sem, in_sem, target):
+        return pltpu.make_async_remote_copy(
+            src_ref=src, dst_ref=dst, send_sem=out_sem, recv_sem=in_sem,
+            device_id=target, device_id_type=pl.DeviceIdType.MESH,
+        )
+
+    order = [k for k in range(1, n)]
+
+    barrier = pltpu.get_barrier_semaphore()
+    for k in range(1, n):
+        pl.semaphore_signal(barrier, inc=1, device_id={"seq": seq(k)}, device_id_type=pl.DeviceIdType.MESH)
+    for k in range(1, replicas):
+        pl.semaphore_signal(barrier, inc=1, device_id={"dp": replica(k)}, device_id_type=pl.DeviceIdType.MESH)
+    own = [
+        pltpu.make_async_copy(x_hbm.at[:, left], x.at[mine, :], scr["own"].at[0]),
+        pltpu.make_async_copy(g_hbm.at[:, left], g.at[mine, :], scr["own"].at[1]),
+    ]
+    for copy in own:
+        copy.start()
+    bk[mine, :] = wk[...]
+    ck[mine, :] = rk[...]
+    raws[mine, :] = raw[...]
+    pl.semaphore_wait(barrier, n + replicas - 2)
+
+    def key_copies(k):
+        target = {"seq": seq(k)}
+        return [
+            send(src, dst.at[mine, :], scr["key_out"].at[k, j], scr["key_in"].at[k, j], target)
+            for j, (src, dst) in enumerate(((wk, bk), (rk, ck), (raw, raws)))
+        ]
+
+    def entry_copies(p, k):
+        target = seq(k)
+        there = pl.ds(pl.multiple_of(target * span + p * LANES, LANES), LANES)
+        here = pl.ds(pl.multiple_of(p * LANES, LANES), LANES)
+        return [
+            send(
+                src.at[:, there], dst.at[mine, here], scr["go_out"].at[p, k, j],
+                scr["go_in"].at[p, k, j], {"seq": target},
+            )
+            for j, (src, dst) in enumerate(((x_hbm, x), (g_hbm, g)))
+        ]
+
+    def exit_copy(p, k):
+        target = seq(k)
+        theirs = pl.ds(pl.multiple_of(target * rows, rows), rows)
+        here = pl.ds(pl.multiple_of(p * LANES, LANES), LANES)
+        there = pl.ds(pl.multiple_of(me * span + p * LANES, LANES), LANES)
+        return send(
+            dx.at[theirs, here], dx_out.at[:, there], scr["back_out"].at[p, k],
+            scr["back_in"].at[p, k], {"seq": target},
+        )
+
+    for k in order:
+        for copy in key_copies(k):
+            copy.start()
+
+    def launch(p, _):
+        for k in order:
+            for copy in entry_copies(p, k):
+                copy.start()
+        return 0
+
+    lax.fori_loop(0, pairs, launch, 0)
+    for k in order:
+        for copy in key_copies(k):
+            copy.wait_recv()
     prepare(
-        raw, decay, bias, scr["wide"], scr["small"], scr["arow"], scr["acol"],
+        raws, me * heads, decay, bias, scr["wide"], scr["small"], scr["arow"], scr["acol"],
         scr["dts"], scr["sig"], scr["rate"], heads,
     )
     scores(bk, ck, scr, length)
     scr["col"][...] = jnp.zeros_like(scr["col"])
-
-    def body(pair, _):
-        one_pair(pair, x, g, skip, dx, scr, length)
+    for copy in own:
+        copy.wait()
+
+    def body(p, _):
+        for k in order:
+            for copy in entry_copies(p, k):
+                copy.wait_recv()
+        one_pair(p, x, g, skip, dx, scr, length)
+        for k in order:
+            exit_copy(p, k).start()
         return 0
 
-    lax.fori_loop(0, heads // 2, body, 0)
-    step_out, par_out = step_grads(scr, heads, length)
-    step[...] = step_out.astype(bf16)
-    par[...] = par_out
+    lax.fori_loop(0, pairs, body, 0)
+    keep = pltpu.make_async_copy(dx.at[mine, :], dx_out.at[:, left], scr["own"].at[2])
+    keep.start()
 
     def write(i, db, dc):
-        rows = slice(i * LANES, (i + 1) * LANES)
-        dkeys[rows, :LANES] = db
-        dkeys[rows, LANES:] = dc
+        here = slice(i * LANES, (i + 1) * LANES)
+        scr["dkeys"][here, :LANES] = db
+        scr["dkeys"][here, LANES:] = dc
 
     key_grads(bk, ck, scr, length, write)
 
-
-def backward(x, raw, bk, ck, g, decay, skip, bias):
-    length, heads = raw.shape
-    space = scratch(heads, length)
+    def sum_copy(k):
+        theirs = pl.ds(pl.multiple_of(seq(k) * rows, rows), rows)
+        return send(
+            scr["dkeys"].at[theirs, :], scr["dk_got"].at[k], scr["dk_out"].at[k],
+            scr["dk_in"].at[k], {"seq": seq(k)},
+        )
+
+    for k in order:
+        sum_copy(k).start()
+    step_all, params = step_grads(scr, heads, length)
+    place = jnp.where(iota((LANES, LANES), 0) + me * heads == iota((LANES, LANES), 1), 1.0, 0.0)
+    place = jnp.where(iota((LANES, LANES), 0) < heads, place, 0.0)
+    scr["step"][...] = dot_nn(step_all.astype(bf16), place.astype(bf16)).astype(bf16)
+    scr["par"][...] = params
+
+    def step_copy(k):
+        theirs = pl.ds(pl.multiple_of(seq(k) * rows, rows), rows)
+        return send(
+            scr["step"].at[theirs, :], scr["step_got"].at[k], scr["st_out"].at[k],
+            scr["st_in"].at[k], {"seq": seq(k)},
+        )
+
+    def par_copy(k):
+        return send(
+            scr["par"], scr["par_got"].at[k], scr["par_out"].at[k], scr["par_in"].at[k],
+            {"dp": replica(k)},
+        )
+
+    for k in range(1, replicas):
+        par_copy(k).start()
+    for k in order:
+        step_copy(k).start()
+
+    total = scr["dkeys"][mine, :]
+    for k in order:
+        sum_copy(k).wait_recv()
+        total = total + scr["dk_got"][k]
+    dwrite[...] = total[:, :LANES].astype(bf16)
+    dread[...] = total[:, LANES:].astype(bf16)
+    steps = scr["step"][mine, :].astype(f32)
+    for k in order:
+        step_copy(k).wait_recv()
+        steps = steps + scr["step_got"][k].astype(f32)
+    step[...] = steps[:, : step.shape[1]].astype(bf16)
+    params = scr["par"][...]
+    for k in range(1, replicas):
+        par_copy(k).wait_recv()
+        params = params + scr["par_got"][k]
+    par[...] = params[:3, :heads] / replicas
+
+    keep.wait()
+
+    def drain(p, _):
+        for k in order:
+            for copy in entry_copies(p, k):
+                copy.wait_send()
+            exit_copy(p, k).wait()
+        return 0
+
+    lax.fori_loop(0, pairs, drain, 0)
+    for k in order:
+        for copy in key_copies(k):
+            copy.wait_send()
+        sum_copy(k).wait_send()
+        step_copy(k).wait_send()
+    for k in range(1, replicas):
+        par_copy(k).wait_send()
+
+
+def backward(n, replicas, x, raw, wk, rk, g, decay, skip, bias):
+    rows, total = raw.shape
+    heads, length = decay.shape[0], rows * n
+    pairs = heads // 2
+    dma = pltpu.SemaphoreType.DMA
+    space = scratch(heads, length) | {
+        "x": pltpu.VMEM((length, pairs * LANES), bf16),
+        "g": pltpu.VMEM((length, pairs * LANES), bf16),
+        "dx": pltpu.VMEM((length, pairs * LANES), bf16),
+        "bk": pltpu.VMEM((length, LANES), bf16),
+        "ck": pltpu.VMEM((length, LANES), bf16),
+        "raws": pltpu.VMEM((length, total), bf16),
+        "dkeys": pltpu.VMEM((length, 2 * LANES), f32),
+        "dk_got": pltpu.VMEM((n, rows, 2 * LANES), f32),
+        "step": pltpu.VMEM((length, LANES), bf16),
+        "step_got": pltpu.VMEM((n, rows, LANES), bf16),
+        "par": pltpu.VMEM((8, LANES), f32),
+        "par_got": pltpu.VMEM((replicas, 8, LANES), f32),
+        "own": dma((3,)),
+        "key_out": dma((n, 3)),
+        "key_in": dma((n, 3)),
+        "go_out": dma((pairs, n, 2)),
+        "go_in": dma((pairs, n, 2)),
+        "back_out": dma((pairs, n)),
+        "back_in": dma((pairs, n)),
+        "dk_out": dma((n,)),
+        "dk_in": dma((n,)),
+        "st_out": dma((n,)),
+        "st_in": dma((n,)),
+        "par_out": dma((replicas,)),
+        "par_in": dma((replicas,)),
+    }
     vmem = pl.BlockSpec(memory_space=pltpu.VMEM)
     smem = pl.BlockSpec(memory_space=pltpu.SMEM)
+    hbm = pl.BlockSpec(memory_space=pl.ANY)
     return pl.pallas_call(
-        functools.partial(kernel, tuple(space), heads, length),
+        functools.partial(kernel, tuple(space), n, replicas),
         out_shape=(
             jax.ShapeDtypeStruct(x.shape, bf16),
             jax.ShapeDtypeStruct(raw.shape, bf16),
-            jax.ShapeDtypeStruct((length, 2 * LANES), f32),
+            jax.ShapeDtypeStruct(wk.shape, bf16),
+            jax.ShapeDtypeStruct(rk.shape, bf16),
             jax.ShapeDtypeStruct((3, heads), f32),
         ),
-        in_specs=[vmem, vmem, vmem, vmem, vmem, vmem, smem, vmem],
-        out_specs=(vmem, vmem, vmem, vmem),
+        in_specs=[hbm, vmem, vmem, vmem, hbm, vmem, smem, vmem],
+        out_specs=(hbm, vmem, vmem, vmem, vmem),
         scratch_shapes=list(space.values()),
-        compiler_params=pltpu.CompilerParams(vmem_limit_bytes=60 * 1024 * 1024),
-    )(x, raw, bk, ck, g, decay.reshape(1, heads), skip, bias.reshape(1, heads))
-
-
-def shards(inputs, raw_step, write_keys, read_keys, grad_out, decay_log, skip_gain, step_bias):
-    replicas = lax.axis_size("dp")
-    swap = functools.partial(lax.all_to_all, axis_name="seq", split_axis=1, concat_axis=0, tiled=True)
-    x, g, raw = swap(inputs[0]), swap(grad_out[0]), swap(raw_step[0])
-    keys = lax.all_gather(jnp.concatenate([write_keys[0], read_keys[0]], axis=1), "seq", axis=0, tiled=True)
-    dx, step, dkeys, par = backward(
-        x, raw, keys[:, :LANES], keys[:, LANES:], g, decay_log, skip_gain, step_bias
+        compiler_params=pltpu.CompilerParams(
+            vmem_limit_bytes=60 * 1024 * 1024, collective_id=0, has_side_effects=True
+        ),
+    )(x, raw, wk, rk, g, decay.reshape(1, heads), skip, bias.reshape(1, heads))
+
+
+def shards(n, replicas, inputs, raw_step, write_keys, read_keys, grad_out, decay_log, skip_gain, step_bias):
+    dx, step, dwrite, dread, par = backward(
+        n, replicas, inputs[0], raw_step[0], write_keys[0], read_keys[0], grad_out[0],
+        decay_log, skip_gain, step_bias,
     )
-    back = functools.partial(lax.all_to_all, axis_name="seq", split_axis=0, concat_axis=1, tiled=True)
-    grad_x, grad_step = back(dx), back(step)
-    summed = lax.psum_scatter(dkeys, "seq", scatter_dimension=0, tiled=True).astype(bf16)
-    total = lax.psum(par, "dp") / replicas
-    return (
-        grad_x[None], grad_step[None], summed[None, :, :LANES], summed[None, :, LANES:], total,
-    )
+    return dx[None], step[None], dwrite[None], dread[None], par
 
 
 def solution(mesh):
     rows = P("dp", "seq", None)
     return jax.shard_map(
-        shards,
+        functools.partial(shards, mesh.shape["seq"], mesh.shape["dp"]),
         mesh=mesh,
         in_specs=(rows,) * 5 + (P("seq"),) * 3,
         out_specs=(rows,) * 4 + (P(None, "seq"),),

time: 115 us -> 64.7 us (0.56)
  blocking collectives: 44.9 us -> 0 us
  Pallas kernels: 14 us -> 56.5 us
  starting transfers between devices: 14.9 us -> 0 us
  between operations: 14.1 us -> 0.64 us
  waiting for transfers between devices: 13.1 us -> 0 us
  local copies, waits for them, and re-layouts: 12.3 us -> 7.18 us
  other arithmetic: 1.51 us -> 0 us
    pallas_call x1, Pallas kernels: 14 us -> 56.5 us  [backward(): pl.pallas_call(functools.partial(kernel, tuple(space), n, replicas), out_...]
    psum x1 -> x0, blocking collectives: 22.1 us -> none  [shards(): total = lax.psum(par, 'dp') / replicas]
    all_gather x1 -> x0, blocking collectives: 16.6 us -> none  [shards(): lax.all_gather(jnp.concatenate([write_keys[0], read_keys[0]], axis=1), 's...]
    all_to_all x4 -> x0, starting transfers between devices: 14.9 us -> none  [the longest x3 11.3 us: shards(): x, g, raw = (swap(inputs[0]), swap(grad_out[0]), swap(raw_step[0]))]
    all_to_all x4 -> x0, waiting for transfers between devices: 13 us -> none  [the longest x3 13 us: shards(): x, g, raw = (swap(inputs[0]), swap(grad_out[0]), swap(raw_step[0]))]
    all_to_all x7 -> x0, local copies, waits for them, and re-layouts: 6.87 us -> none  [the longest x5 5.98 us: shards(): x, g, raw = (swap(inputs[0]), swap(grad_out[0]), swap(raw_step[0]))]
    all_to_all x1 -> x0, blocking collectives: 6.21 us -> none  [shards(): grad_x, grad_step = (back(dx), back(step))]
    unnamed x15 -> x12, local copies, waits for them, and re-layouts: 2.5 us -> 7.18 us
  transfers between devices with their start and end apart: 5 -> 0, of which waited for: 2 -> 0; matrix products, arithmetic and copies ran while one was open for 6% -> 0% of each run, Pallas kernels for 0% -> 0%
where the time goes in v1:
time: 64.7 us; the launch traced here: 64.3 us
  Pallas kernels  56.5 us (87%)
  local copies, waits for them, and re-layouts  7.18 us (11%)
    pallas_call x1, Pallas kernels, backward(): pl.pallas_call(functools.partial(kernel, tuple(space), n, replicas), out_...  56.5 us
    unnamed x12, local copies, waits for them, and re-layouts  7.18 us

profile of v1, /device:TPU:0, one launch (start us, length us, event | category | flops | bytes accessed | tf_op | source)
XLA Modules:
  0.0 64.3 jit_solution(12704031561302371574)
XLA Ops:
  0.6 1.4 %copy.13 = bf16[1,128,64]{2,1,0:T(8,128)(2,1)} copy(bf16[1,128,64]{1,2,0:T(8,128)(2,1)} %param.9) | data formatting | bytes 32768 | tf_op args[1]
  2.1 56.5 %shard_map.119 = (bf16[128,4096]{1,0:T(8,128)(2,1)}, bf16[128,64]{1,0:T(8,128)(2,1)}, bf16[128,128]{1,0:T(8,128)(2,1)}, bf16[128,128]{1,0:T(8,128)(2,1)}, f32[3,16]{1,0:T(4,128)}) custom-call(bf16[128,4096]{1,0:T(8,128)(2,1)} %bitcast.11, bf16[128,64]{1,0:T(8,128)(2,1)} %bitcast.14, bf16[128,128]{1,0:T(8,128)(2,1)} %bitcast.15, bf16[128,128]{1,0:T(8,128)(2,1)} %bitcast.16, ...), custom_call_target="tpu_custom_call" | custom-call | tf_op jit(solution)/shard_map/pallas_call | solution.py:456
  58.5 1.4 %copy.14 = bf16[1,128,64]{1,2,0:T(8,128)(2,1)} copy(bf16[1,128,64]{2,1,0:T(8,128)(2,1)} %bitcast.17) | data formatting | bytes 32768
  60.0 0.0 copy-start.1
  60.0 2.3 %copy.19 = bf16[1,128,4096]{2,1,0:T(8,128)(2,1)} copy(bf16[1,128,4096]{2,1,0:T(8,128)(2,1)} %bitcast.13) | data formatting | bytes 2097152
  62.3 0.0 copy-done.1
  62.3 0.0 copy-start
  62.3 0.6 copy.20
  62.9 0.2 copy-done
  63.1 0.0 copy-start.2
  63.1 0.6 copy.21
  63.7 0.0 copy-done.2
  63.7 0.6 copy.22
Async XLA Ops:
  60.0 2.3 %copy-start.1 = (bf16[128,128]{1,0:T(8,128)(2,1)S(1)}, bf16[128,128]{1,0:T(8,128)(2,1)}, u32[]{:S(2)}) copy-start(bf16[128,128]{1,0:T(8,128)(2,1)} %get-tuple-element.12) | copy-start | bytes 98308
  62.3 0.8 %copy-start = (bf16[128,128]{1,0:T(8,128)(2,1)S(1)}, bf16[128,128]{1,0:T(8,128)(2,1)}, u32[]{:S(2)}) copy-start(bf16[128,128]{1,0:T(8,128)(2,1)} %get-tuple-element.13) | copy-start | bytes 98308
  63.1 0.7 %copy-start.2 = (f32[3,16]{1,0:T(4,128)S(1)}, f32[3,16]{1,0:T(4,128)}, u32[]{:S(2)}) copy-start(f32[3,16]{1,0:T(4,128)} %get-tuple-element.29) | copy-start | bytes 580

commit v2 on v1

v2 whole, which is shorter than its diff:
```python
import functools
import types

import jax
import jax.numpy as jnp
from jax import lax
from jax.experimental import pallas as pl
from jax.experimental.pallas import tpu as pltpu
from jax.sharding import PartitionSpec as P

LANES = 128
ROWS = 16
LOG2E = 1.4426950408889634
bf16 = jnp.bfloat16
f32 = jnp.float32


def iota(shape, dim):
    return lax.broadcasted_iota(jnp.int32, shape, dim)


def dot_nt(a, b):
    return lax.dot_general(a, b, (((1,), (1,)), ((), ())), preferred_element_type=f32)


def dot_nn(a, b):
    return jnp.dot(a, b, preferred_element_type=f32)


def split_two(v):
    hi = v.astype(bf16)
    return hi, (v - hi.astype(f32)).astype(bf16)


def scan_lanes(v, reverse):
    rows, length = v.shape
    width = min(256, length)
    r, c = iota((width, width), 0), iota((width, width), 1)
    keep = (r >= c) if reverse else (r <= c)
    ones = jnp.where(keep, 1.0, 0.0).astype(bf16)
    one = v.astype(bf16)
    rest = v - one.astype(f32)
    two = rest.astype(bf16)
    three = (rest - two.astype(f32)).astype(bf16)
    stacked = jnp.concatenate([one, two, three], axis=0)
    spots = list(range(0, length, width))
    carry = jnp.zeros((rows, 1), f32)
    out = {}
    for start in reversed(spots) if reverse else spots:
        part = dot_nn(stacked[:, start : start + width], ones)
        part = part[:rows] + (part[rows : 2 * rows] + part[2 * rows :]) + carry
        out[start] = part
        carry = part[:, :1] if reverse else part[:, width - 1 :]
    return jnp.concatenate([out[s] for s in spots], axis=1)


def column(small, row, heads):
    small[0:1, :heads] = row
    return jnp.broadcast_to(small[0:1, :], (LANES, LANES)).T[:heads]


def pick_heads(raws, offset, heads):
    n, total, _ = raws.shape
    pick = jnp.where(iota((heads, total), 1) == iota((heads, total), 0) + offset, 1.0, 0.0)
    return jnp.concatenate([dot_nn(pick.astype(bf16), raws[k]) for k in range(n)], axis=1)


def prepare(z, decay, bias, small, arow, acol, dts, sig, rate, heads):
    length = z.shape[1]
    small[...] = jnp.zeros_like(small)
    z = z + column(small, bias, heads)[:, :1]
    rate_col = column(small, jnp.exp(decay), heads)
    rate[...] = rate_col
    dt = jnp.maximum(z, 0.0) + jnp.log1p(jnp.exp(-jnp.abs(z)))
    dts[...] = dt
    sig[...] = 1.0 / (1.0 + jnp.exp(-z))
    a = scan_lanes(dt * (rate_col[:, :1] * -LOG2E), False)
    for h in range(heads):
        arow[h] = jnp.broadcast_to(a[h : h + 1, :], (8, length))
    below = a - jnp.log(dt) * LOG2E
    down = jnp.concatenate([below, jnp.zeros((LANES - heads, length), f32)], axis=0).T
    for h in range(heads):
        acol[h] = jnp.broadcast_to(down[:, h : h + 1], (length, LANES))


def tile(pair, s0, t0, width, diagonal, x, g, scr):
    w, m, vacc = scr.w, scr.m, scr.vacc
    lanes = pl.ds(pl.multiple_of(pair * LANES, LANES), LANES)
    srows, trows = pl.ds(s0, LANES), pl.ds(t0, width)
    xs = x[srows, lanes]
    gs = g[trows, lanes]
    low = iota((width, LANES), 1) < LANES // 2
    zero = jnp.zeros_like(gs)
    parts = (jnp.where(low, gs, zero), jnp.where(low, zero, gs))
    for k in range(2):
        w[k, :, :width] = dot_nt(xs, parts[k])
    lane = iota((ROWS, LANES), 1)
    at = [scr.arow[2 * pair + k, :, trows] for k in range(2)]
    at = [jnp.concatenate([v] * (ROWS // 8), axis=0) for v in at]
    sums = [None, None]
    for c in range(LANES // ROWS):
        rows = pl.ds(s0 + c * ROWS, ROWS)
        here = slice(c * ROWS, (c + 1) * ROWS)
        s_tile = scr.score[rows, trows]
        q = scr.q[rows, trows]
        col = scr.col[rows, :]
        for k in range(2):
            ac = scr.acol[2 * pair + k, rows, :]
            gap = at[k] - jnp.concatenate([ac] * (width // LANES), axis=1)
            if diagonal:
                keep = iota((ROWS, width), 1) >= iota((ROWS, width), 0) + c * ROWS
                gap = jnp.where(keep, gap, -jnp.inf)
            lp = jnp.exp2(gap)
            wk = w[k, here, :width]
            q = q + lp * wk
            mk = lp * s_tile
            hi, lo = split_two(mk)
            m[2 * k, here, :width] = hi
            m[2 * k + 1, here, :width] = lo
            zk = mk * wk
            part = zk[:8] + zk[8:]
            sums[k] = part if sums[k] is None else sums[k] + part
            across = zk[:, :LANES]
            for j in range(1, width // LANES):
                across = across + zk[:, j * LANES : (j + 1) * LANES]
            total = jnp.sum(across, axis=1, keepdims=True)
            col = col + jnp.where(lane == 2 * pair + k, total, 0.0)
        scr.q[rows, trows] = q
        scr.col[rows, :] = col
    for k in range(2):
        scr.racc[k, :, trows] += sums[k]
    v = None
    for k in range(2):
        for j in range(2):
            term = dot_nn(m[2 * k + j, :, :width], parts[k])
            v = term if v is None else v + term
    return v


def one_pair(pair, x, g, gain, dx, scr, length):
    lanes = pl.ds(pl.multiple_of(pair * LANES, LANES), LANES)
    scr.racc[...] = jnp.zeros_like(scr.racc)
    low = iota((1, LANES), 1) < LANES // 2
    blocks = length // LANES

    def finish(s0, v):
        rows = pl.ds(s0, LANES)
        gs = g[rows, lanes].astype(f32)
        dx[rows, lanes] = (v + gain * gs).astype(dx.dtype)
        scr.direct[...] += jnp.sum(
            (x[rows, lanes].astype(f32) * gs).reshape(LANES // 8, 8, LANES), axis=0
        )

    scr.direct[...] = jnp.zeros_like(scr.direct)
    if blocks <= 4:
        for i in range(blocks):
            s0 = i * LANES
            finish(s0, tile(pair, s0, s0, length - s0, True, x, g, scr))
    else:

        def block(i, _):
            s0 = pl.multiple_of(i * LANES, LANES)
            scr.vacc[...] = tile(pair, s0, s0, LANES, True, x, g, scr)

            def right(j, _):
                t0 = pl.multiple_of(j * LANES, LANES)
                scr.vacc[...] += tile(pair, s0, t0, LANES, False, x, g, scr)
                return 0

            lax.fori_loop(i + 1, blocks, right, 0)
            finish(s0, scr.vacc[...])
            return 0

        lax.fori_loop(0, blocks, block, 0)
    direct = jnp.sum(scr.direct[...], axis=0, keepdims=True)
    for k in range(2):
        scr.row[pl.ds(2 * pair + k, 1), :] = jnp.sum(scr.racc[k], axis=0, keepdims=True)
        mine = jnp.where(low, direct, 0.0) if k == 0 else jnp.where(low, 0.0, direct)
        scr.gain[pl.ds(2 * pair + k, 1), :] = jnp.broadcast_to(
            jnp.sum(mine, axis=1, keepdims=True), (1, LANES)
        )


def scores(bk, ck, scr, length):
    blocks = length // LANES
    for i in range(blocks):
        s0 = i * LANES
        scr.score[s0 : s0 + LANES, s0:] = dot_nt(bk[s0 : s0 + LANES, :], ck[s0:, :])
        scr.q[s0 : s0 + LANES, s0:] = jnp.zeros((LANES, length - s0), f32)


def step_grads(scr, heads, length, cross=None):
    col = scr.col[...].T[:heads]
    row = scr.row[...]
    extra = 0.0
    if cross is not None:
        first, value = cross
        value = value.T[:heads]
        col = col + jnp.where(first, value, 0.0)
        row = row + jnp.where(first, 0.0, value)
        extra = jnp.where(first, jnp.sum(value, axis=1, keepdims=True), 0.0)
    dl = scan_lanes(row - col, True) + extra
    rate = scr.rate[:, :1]
    dt = scr.dts[...]
    ddt = col / dt - rate * dl
    draw = ddt * scr.sig[...]
    decay = -rate * jnp.sum(dl * dt, axis=1, keepdims=True)
    shift = jnp.sum(draw, axis=1, keepdims=True)
    lane = iota((heads, LANES), 1)
    params = jnp.where(lane == 0, decay, jnp.where(lane == 1, scr.gain[...], shift))
    params = jnp.concatenate([params, jnp.zeros((LANES - heads, LANES), f32)], axis=0).T
    return draw, params[:8]


def key_grads(bk, ck, scr, length, write):
    blocks = length // LANES
    bt = bk[...].astype(f32).T.astype(bf16)
    for i in range(blocks):
        here = slice(i * LANES, (i + 1) * LANES)
        hi, lo = split_two(scr.q[here, i * LANES :])
        db = dot_nn(hi, ck[i * LANES :, :]) + dot_nn(lo, ck[i * LANES :, :])
        upto = (i + 1) * LANES
        hi, lo = split_two(scr.q[:upto, here])
        dc = dot_nn(bt[:, :upto], hi) + dot_nn(bt[:, :upto], lo)
        write(i, db, dc.T)


def scratch(heads, length):
    width = length if length <= 4 * LANES else LANES
    return dict(
        small=pltpu.VMEM((8, LANES), f32),
        arow=pltpu.VMEM((heads, 8, length), f32),
        acol=pltpu.VMEM((heads, length, LANES), f32),
        dts=pltpu.VMEM((heads, length), f32),
        sig=pltpu.VMEM((heads, length), f32),
        rate=pltpu.VMEM((heads, LANES), f32),
        score=pltpu.VMEM((length, length), f32),
        q=pltpu.VMEM((length, length), f32),
        col=pltpu.VMEM((length, LANES), f32),
        row=pltpu.VMEM((heads, length), f32),
        gain=pltpu.VMEM((heads, LANES), f32),
        racc=pltpu.VMEM((2, 8, length), f32),
        direct=pltpu.VMEM((8, LANES), f32),
        vacc=pltpu.VMEM((LANES, LANES), f32),
        w=pltpu.VMEM((2, LANES, width), f32),
        m=pltpu.VMEM((4, LANES, width), bf16),
    )


def kernel(names, n, replicas, x_hbm, raw, wk, rk, g_hbm, decay, skip, bias, dx_out, step, dwrite, dread, par, *rest):
    scr = types.SimpleNamespace(**dict(zip(names, rest)))
    rows = x_hbm.shape[0]
    length = rows * n
    heads = decay.shape[1]
    pairs = heads // 2
    span = pairs * LANES
    me, dp = lax.axis_index("seq"), lax.axis_index("dp")
    x, g, dx, bk, ck, raws = (scr.x, scr.g, scr.dx, scr.bk, scr.ck, scr.raws)
    mine = pl.ds(pl.multiple_of(me * rows, rows), rows)
    left = pl.ds(pl.multiple_of(me * span, span), span)

    def seq(k):
        return lax.rem(me + k, n)

    def replica(k):
        return lax.rem(dp + k, replicas)

    def send(src, dst, out_sem, in_sem, target):
        return pltpu.make_async_remote_copy(
            src_ref=src, dst_ref=dst, send_sem=out_sem, recv_sem=in_sem,
            device_id=target, device_id_type=pl.DeviceIdType.MESH,
        )

    order = [k for k in range(1, n)]

    barrier = pltpu.get_barrier_semaphore()
    for k in range(1, n):
        pl.semaphore_signal(barrier, inc=1, device_id={"seq": seq(k)}, device_id_type=pl.DeviceIdType.MESH)
    for k in range(1, replicas):
        pl.semaphore_signal(barrier, inc=1, device_id={"dp": replica(k)}, device_id_type=pl.DeviceIdType.MESH)
    own = [
        pltpu.make_async_copy(x_hbm.at[:, left], x.at[mine, :], scr.own.at[0]),
        pltpu.make_async_copy(g_hbm.at[:, left], g.at[mine, :], scr.own.at[1]),
    ]
    for copy in own:
        copy.start()
    bk[mine, :] = wk[...]
    ck[mine, :] = rk[...]
    raws[me] = raw[...]
    pl.semaphore_wait(barrier, n + replicas - 2)

    def key_copies(k):
        target = {"seq": seq(k)}
        return [
            send(src, dst, scr.key_out.at[k, j], scr.key_in.at[k, j], target)
            for j, (src, dst) in enumerate(((wk, bk.at[mine, :]), (rk, ck.at[mine, :]), (raw, raws.at[me])))
        ]

    def entry_copies(p, k):
        target = seq(k)
        there = pl.ds(pl.multiple_of(target * span + p * LANES, LANES), LANES)
        here = pl.ds(pl.multiple_of(p * LANES, LANES), LANES)
        return [
            send(
                src.at[:, there], dst.at[mine, here], scr.go_out.at[p, k, j],
                scr.go_in.at[p, k, j], {"seq": target},
            )
            for j, (src, dst) in enumerate(((x_hbm, x), (g_hbm, g)))
        ]

    def exit_copy(p, k):
        target = seq(k)
        theirs = pl.ds(pl.multiple_of(target * rows, rows), rows)
        here = pl.ds(pl.multiple_of(p * LANES, LANES), LANES)
        there = pl.ds(pl.multiple_of(me * span + p * LANES, LANES), LANES)
        return send(
            dx.at[theirs, here], dx_out.at[:, there], scr.back_out.at[p, k],
            scr.back_in.at[p, k], {"seq": target},
        )

    for k in order:
        for copy in key_copies(k):
            copy.start()

    def launch(p, _):
        for k in order:
            for copy in entry_copies(p, k):
                copy.start()
        return 0

    lax.fori_loop(0, pairs, launch, 0)
    for k in order:
        for copy in key_copies(k):
            copy.wait_recv()
    prepare(
        pick_heads(raws, me * heads, heads), decay[...], bias[...], scr.small, scr.arow, scr.acol,
        scr.dts, scr.sig, scr.rate, heads,
    )
    scores(bk, ck, scr, length)
    scr.col[...] = jnp.zeros_like(scr.col)
    for copy in own:
        copy.wait()

    def body(p, _):
        for k in order:
            for copy in entry_copies(p, k):
                copy.wait_recv()
        low = iota((1, LANES), 1) < LANES // 2
        gain = jnp.where(low, skip[2 * p], skip[2 * p + 1])
        one_pair(p, x, g, gain, dx, scr, length)
        for k in order:
            exit_copy(p, k).start()
        return 0

    lax.fori_loop(0, pairs, body, 0)
    keep = pltpu.make_async_copy(dx.at[mine, :], dx_out.at[:, left], scr.own.at[2])
    keep.start()

    def write(i, db, dc):
        here = slice(i * LANES, (i + 1) * LANES)
        scr.dkeys[here, :LANES] = db
        scr.dkeys[here, LANES:] = dc

    key_grads(bk, ck, scr, length, write)

    def sum_copy(k):
        theirs = pl.ds(pl.multiple_of(seq(k) * rows, rows), rows)
        return send(
            scr.dkeys.at[theirs, :], scr.dk_got.at[k], scr.dk_out.at[k],
            scr.dk_in.at[k], {"seq": seq(k)},
        )

    for k in order:
        sum_copy(k).start()
    step_all, params = step_grads(scr, heads, length)
    spread = (raw.shape[0], heads)
    place = jnp.where(iota(spread, 1) + me * heads == iota(spread, 0), 1.0, 0.0)
    scr.step[...] = dot_nn(place.astype(bf16), step_all.astype(bf16)).astype(bf16)
    scr.par[...] = params

    def step_copy(k):
        theirs = pl.ds(pl.multiple_of(seq(k) * rows, rows), rows)
        return send(
            scr.step.at[:, theirs], scr.step_got.at[k], scr.st_out.at[k],
            scr.st_in.at[k], {"seq": seq(k)},
        )

    def par_copy(k):
        return send(
            scr.par, scr.par_got.at[k], scr.par_out.at[k], scr.par_in.at[k],
            {"dp": replica(k)},
        )

    for k in range(1, replicas):
        par_copy(k).start()
    for k in order:
        step_copy(k).start()

    total = scr.dkeys[mine, :]
    for k in order:
        sum_copy(k).wait_recv()
        total = total + scr.dk_got[k]
    dwrite[...] = total[:, :LANES].astype(bf16)
    dread[...] = total[:, LANES:].astype(bf16)
    steps = scr.step[:, mine].astype(f32)
    for k in order:
        step_copy(k).wait_recv()
        steps = steps + scr.step_got[k].astype(f32)
    step[...] = steps.astype(bf16)
    params = scr.par[...]
    for k in range(1, replicas):
        par_copy(k).wait_recv()
        params = params + scr.par_got[k]
    par[...] = params[:3, :heads] / replicas

    keep.wait()

    def drain(p, _):
        for k in order:
            for copy in entry_copies(p, k):
                copy.wait_send()
            exit_copy(p, k).wait()
        return 0

    lax.fori_loop(0, pairs, drain, 0)
    for k in order:
        for copy in key_copies(k):
            copy.wait_send()
        sum_copy(k).wait_send()
        step_copy(k).wait_send()
    for k in range(1, replicas):
        par_copy(k).wait_send()


def backward(n, replicas, x, raw, wk, rk, g, decay, skip, bias):
    total, rows = raw.shape
    heads, length = decay.shape[0], rows * n
    pairs = heads // 2
    dma = pltpu.SemaphoreType.DMA
    space = scratch(heads, length) | dict(
        x=pltpu.VMEM((length, pairs * LANES), bf16),
        g=pltpu.VMEM((length, pairs * LANES), bf16),
        dx=pltpu.VMEM((length, pairs * LANES), bf16),
        bk=pltpu.VMEM((length, LANES), bf16),
        ck=pltpu.VMEM((length, LANES), bf16),
        raws=pltpu.VMEM((length // rows, total, rows), bf16),
        dkeys=pltpu.VMEM((length, 2 * LANES), f32),
        dk_got=pltpu.VMEM((n, rows, 2 * LANES), f32),
        step=pltpu.VMEM((total, length), bf16),
        step_got=pltpu.VMEM((n, total, rows), bf16),
        par=pltpu.VMEM((8, LANES), f32),
        par_got=pltpu.VMEM((replicas, 8, LANES), f32),
        own=dma((3,)),
        key_out=dma((n, 3)),
        key_in=dma((n, 3)),
        go_out=dma((pairs, n, 2)),
        go_in=dma((pairs, n, 2)),
        back_out=dma((pairs, n)),
        back_in=dma((pairs, n)),
        dk_out=dma((n,)),
        dk_in=dma((n,)),
        st_out=dma((n,)),
        st_in=dma((n,)),
        par_out=dma((replicas,)),
        par_in=dma((replicas,)),
    )
    vmem = pl.BlockSpec(memory_space=pltpu.VMEM)
    smem = pl.BlockSpec(memory_space=pltpu.SMEM)
    hbm = pl.BlockSpec(memory_space=pl.ANY)
    return pl.pallas_call(
        functools.partial(kernel, tuple(space), n, replicas),
        out_shape=(
            jax.ShapeDtypeStruct(x.shape, bf16),
            jax.ShapeDtypeStruct(raw.shape, bf16),
            jax.ShapeDtypeStruct(wk.shape, bf16),
            jax.ShapeDtypeStruct(rk.shape, bf16),
            jax.ShapeDtypeStruct((3, heads), f32),
        ),
        in_specs=[hbm, vmem, vmem, vmem, hbm, vmem, smem, vmem],
        out_specs=(hbm, vmem, vmem, vmem, vmem),
        scratch_shapes=list(space.values()),
        compiler_params=pltpu.CompilerParams(
            vmem_limit_bytes=60 * 1024 * 1024, collective_id=0, has_side_effects=True
        ),
    )(x, raw, wk, rk, g, decay.reshape(1, heads), skip, bias.reshape(1, heads))


def chip_kernel(names, n, replicas, x_hbm, raw, wk, rk, g_hbm, decay, skip, bias, dx_out, step, dwrite, dread, par, *rest):
    scr = types.SimpleNamespace(**dict(zip(names, rest)))
    rows = x_hbm.shape[0]
    length = 2 * rows
    few = decay.shape[1]
    heads = 2 * few
    pairs = heads // 2
    span = pairs * LANES
    me, dp = lax.axis_index("seq"), lax.axis_index("dp")
    chip, core = me // 2, lax.rem(me, 2)
    first = chip == 0
    near, far = me + 1 - 2 * core, lax.rem(me + 2, n)
    x, g, bk, ck, raws = (scr.x, scr.g, scr.bk, scr.ck, scr.raws)
    dxf, dx = scr.dxf, scr.dx
    mine = pl.ds(pl.multiple_of(core * rows, rows), rows)
    theirs = pl.ds(pl.multiple_of((1 - core) * rows, rows), rows)
    left = pl.ds(pl.multiple_of(core * span, span), span)
    mesh_id = pl.DeviceIdType.MESH

    def seq(k):
        return lax.rem(me + k, n)

    def replica(k):
        return lax.rem(dp + k, replicas)

    def send(src, dst, name, at, target):
        return pltpu.make_async_remote_copy(
            src_ref=src, dst_ref=dst, send_sem=getattr(scr, name + "_out").at[at],
            recv_sem=getattr(scr, name + "_in").at[at], device_id=target, device_id_type=mesh_id,
        )

    barrier = pltpu.get_barrier_semaphore()
    for k in range(1, n):
        pl.semaphore_signal(barrier, inc=1, device_id={"seq": seq(k)}, device_id_type=mesh_id)
    for k in range(1, replicas):
        pl.semaphore_signal(barrier, inc=1, device_id={"dp": replica(k)}, device_id_type=mesh_id)
    own = [
        pltpu.make_async_copy(x_hbm.at[:, left], x.at[mine, :], scr.own.at[0]),
        pltpu.make_async_copy(g_hbm.at[:, left], g.at[mine, :], scr.own.at[1]),
    ]
    for copy in own:
        copy.start()
    bk[mine, :] = wk[...]
    ck[mine, :] = rk[...]
    raws[core] = raw[...]
    stage = scr.stage
    stage[...] = jnp.zeros_like(stage)
    stage[0:1, :few] = decay[...]
    stage[1:2, :few] = skip[...]
    stage[2:3, :few] = bias[...]
    scr.prm_got[me] = stage[...]
    pl.semaphore_wait(barrier, n + replicas - 2)

    def prm_copy(k):
        return send(stage, scr.prm_got.at[me], "prm", k, {"seq": seq(k)})

    key_copies = [
        send(src, dst, "key", j, {"seq": near})
        for j, (src, dst) in enumerate(((wk, bk.at[mine, :]), (rk, ck.at[mine, :]), (raw, raws.at[core])))
    ]

    def entry_copies(p):
        there = pl.ds(pl.multiple_of(near % 2 * span + p * LANES, LANES), LANES)
        here = pl.ds(pl.multiple_of(p * LANES, LANES), LANES)
        return [
            send(x_hbm.at[:, there], x.at[mine, here], "gox", p, {"seq": near}),
            send(g_hbm.at[:, there], g.at[mine, here], "gog", p, {"seq": near}),
        ]

    def state_copy(p):
        return send(scr.state.at[p], scr.state_got.at[p], "state", p, {"seq": far})

    def exit_copy(p):
        here = pl.ds(pl.multiple_of(p * LANES, LANES), LANES)
        there = pl.ds(pl.multiple_of(core * span + p * LANES, LANES), LANES)
        return send(dx.at[theirs, here], dx_out.at[:, there], "back", p, {"seq": near})

    for k in range(1, n):
        prm_copy(k).start()
    for copy in key_copies:
        copy.start()

    def launch(p, _):
        for copy in entry_copies(p):
            copy.start()
        return 0

    lax.fori_loop(0, pairs, launch, 0)
    for k in range(1, n):
        prm_copy(k).wait_recv()
    for copy in key_copies:
        copy.wait_recv()
    prm = scr.prm
    prm[...] = jnp.zeros_like(prm)
    prm[:, :few] = scr.prm_got[2 * core][:, :few]
    prm[:, few:heads] = scr.prm_got[2 * core + 1][:, :few]
    prepare(
        pick_heads(raws, core * heads, heads), prm[0:1, :heads], prm[2:3, :heads], scr.small,
        scr.arow, scr.acol, scr.dts, scr.sig, scr.rate, heads,
    )
    gains = jnp.broadcast_to(prm[1:2, :], (LANES, LANES)).T
    for h in range(heads):
        scr.skips[h] = jnp.broadcast_to(gains[h : h + 1, :], (8, LANES))
    a = jnp.concatenate([scr.arow[h, 0:1, :] for h in range(heads)], axis=0)
    tail = a[:, length - 1 :] - a + jnp.log(scr.dts[...]) * LOG2E
    reach = jnp.exp2(jnp.where(first, tail, a))
    reach = jnp.concatenate([reach, jnp.zeros((LANES - heads, length), f32)], axis=0).T
    for h in range(heads):
        scr.reach[h] = jnp.broadcast_to(reach[:, h : h + 1], (length, LANES))
    key = jnp.where(first, bk[...].astype(f32), ck[...].astype(f32))
    scr.key[...] = key.astype(bf16)
    scr.keyt[...] = key.T.astype(bf16)
    for copy in own:
        copy.wait()
    low = iota((length, LANES), 1) < LANES // 2
    low_row = iota((1, LANES), 1) < LANES // 2

    def weigh(p):
        here = pl.ds(pl.multiple_of(p * LANES, LANES), LANES)
        reach = jnp.where(low, scr.reach[2 * p], scr.reach[2 * p + 1])
        value = jnp.where(first, x[:, here].astype(f32), g[:, here].astype(f32))
        return here, reach, value

    def states(p, _):
        for copy in entry_copies(p):
            copy.wait_recv()
        _, reach, value = weigh(p)
        hi, lo = split_two(reach * value)
        kt = scr.keyt[...]
        scr.state[p] = dot_nn(kt, hi) + dot_nn(kt, lo)
        state_copy(p).start()
        return 0

    lax.fori_loop(0, pairs, states, 0)
    scores(bk, ck, scr, length)
    scr.col[...] = jnp.zeros_like(scr.col)

    def inside(p, _):
        gain = jnp.where(low_row, scr.skips[2 * p][0:1], scr.skips[2 * p + 1][0:1])
        one_pair(p, x, g, gain, dxf, scr, length)
        return 0

    lax.fori_loop(0, pairs, inside, 0)

    def write(i, db, dc):
        here = slice(i * LANES, (i + 1) * LANES)
        scr.dkeys[here, :LANES] = db
        scr.dkeys[here, LANES:] = dc

    key_grads(bk, ck, scr, length, write)
    scr.kcross[...] = jnp.zeros_like(scr.kcross)
    scr.zcross[...] = jnp.zeros_like(scr.zcross)
    lane = iota((length, LANES), 1)

    def across(p, _):
        state_copy(p).wait_recv()
        here, reach, value = weigh(p)
        shi, slo = split_two(scr.state_got[p])
        k = scr.key[...]
        u = reach * (dot_nn(k, shi) + dot_nn(k, slo))
        whi, wlo = split_two(reach * value)
        scr.kcross[...] += dot_nt(whi, shi) + (dot_nt(whi, slo) + dot_nt(wlo, shi))
        both = value * u
        one = jnp.sum(jnp.where(low, both, 0.0), axis=1, keepdims=True)
        two = jnp.sum(jnp.where(low, 0.0, both), axis=1, keepdims=True)
        scr.zcross[...] += jnp.where(lane == 2 * p, one, 0.0) + jnp.where(lane == 2 * p + 1, two, 0.0)
        dx[:, here] = (dxf[:, here] + jnp.where(first, u, 0.0)).astype(bf16)
        exit_copy(p).start()
        return 0

    lax.fori_loop(0, pairs, across, 0)
    keep = pltpu.make_async_copy(dx.at[mine, :], dx_out.at[:, left], scr.own.at[2])
    keep.start()
    kcross = scr.kcross[...]
    scr.dkeys[:, :LANES] += jnp.where(first, kcross, 0.0)
    scr.dkeys[:, LANES:] += jnp.where(first, 0.0, kcross)
    sum_copy = send(scr.dkeys.at[theirs, :], scr.dk_got, "dk", 0, {"seq": near})
    sum_copy.start()
    step_all, params = step_grads(scr, heads, length, (first, scr.zcross[...]))
    scr.par[...] = params

    def par_copy(k):
        return send(scr.par, scr.par_got.at[k], "par", k, {"dp": replica(k)})

    for k in range(1, replicas):
        par_copy(k).start()
    held = pl.ds(pl.multiple_of(core * heads, heads), heads)
    scr.step[...] = step_all.astype(bf16)
    step[held, :] = scr.step[:, mine]
    step_copy = send(scr.step.at[:, theirs], step.at[held, :], "st", 0, {"seq": near})
    step_copy.start()
    params = scr.par[...]
    for k in range(1, replicas):
        par_copy(k).wait_recv()
        params = params + scr.par_got[k]
    scr.tot[...] = params
    scr.tot_got[me] = params

    def tot_copy(k):
        return send(scr.tot, scr.tot_got.at[me], "tot", k, {"seq": seq(k)})

    for k in range(1, n):
        tot_copy(k).start()
    sum_copy.wait_recv()
    total = scr.dkeys[mine, :] + scr.dk_got[...]
    dwrite[...] = total[:, :LANES].astype(bf16)
    dread[...] = total[:, LANES:].astype(bf16)
    step_copy.wait_recv()
    for k in range(1, n):
        tot_copy(k).wait_recv()
    params = scr.tot_got[chip] + scr.tot_got[2 + chip]
    par[...] = jnp.where(core == 0, params[:3, :few], params[:3, few:heads]) / replicas
    keep.wait()

    def drain(p, _):
        for copy in entry_copies(p):
            copy.wait_send()
        state_copy(p).wait_send()
        exit_copy(p).wait()
        return 0

    lax.fori_loop(0, pairs, drain, 0)
    for copy in key_copies + [sum_copy, step_copy]:
        copy.wait_send()
    for k in range(1, n):
        prm_copy(k).wait_send()
        tot_copy(k).wait_send()
    for k in range(1, replicas):
        par_copy(k).wait_send()


def chip_backward(n, replicas, x, raw, wk, rk, g, decay, skip, bias):
    total, rows = raw.shape
    few = decay.shape[0]
    heads, length = 2 * few, 2 * rows
    pairs = heads // 2
    space = scratch(heads, length) | dict(
        x=pltpu.VMEM((length, pairs * LANES), bf16),
        g=pltpu.VMEM((length, pairs * LANES), bf16),
        dx=pltpu.VMEM((length, pairs * LANES), bf16),
        dxf=pltpu.VMEM((length, pairs * LANES), f32),
        bk=pltpu.VMEM((length, LANES), bf16),
        ck=pltpu.VMEM((length, LANES), bf16),
        key=pltpu.VMEM((length, LANES), bf16),
        keyt=pltpu.VMEM((LANES, length), bf16),
        raws=pltpu.VMEM((length // rows, total, rows), bf16),
        reach=pltpu.VMEM((heads, length, LANES), f32),
        skips=pltpu.VMEM((heads, 8, LANES), f32),
        state=pltpu.VMEM((pairs, LANES, LANES), f32),
        state_got=pltpu.VMEM((pairs, LANES, LANES), f32),
        kcross=pltpu.VMEM((length, LANES), f32),
        zcross=pltpu.VMEM((length, LANES), f32),
        dkeys=pltpu.VMEM((length, 2 * LANES), f32),
        dk_got=pltpu.VMEM((rows, 2 * LANES), f32),
        step=pltpu.VMEM((heads, length), bf16),
        stage=pltpu.VMEM((8, LANES), f32),
        prm=pltpu.VMEM((8, LANES), f32),
        prm_got=pltpu.VMEM((n, 8, LANES), f32),
        par=pltpu.VMEM((8, LANES), f32),
        par_got=pltpu.VMEM((replicas, 8, LANES), f32),
        tot=pltpu.VMEM((8, LANES), f32),
        tot_got=pltpu.VMEM((n, 8, LANES), f32),
        own=pltpu.SemaphoreType.DMA((3,)),
    )
    counts = dict(
        prm=n, key=3, gox=pairs, gog=pairs, state=pairs, back=pairs, dk=1, st=1, par=replicas, tot=n
    )
    for name, count in counts.items():
        space[name + "_out"] = pltpu.SemaphoreType.DMA((count,))
        space[name + "_in"] = pltpu.SemaphoreType.DMA((count,))
    vmem = pl.BlockSpec(memory_space=pltpu.VMEM)
    hbm = pl.BlockSpec(memory_space=pl.ANY)
    return pl.pallas_call(
        functools.partial(chip_kernel, tuple(space), n, replicas),
        out_shape=(
            jax.ShapeDtypeStruct(x.shape, bf16),
            jax.ShapeDtypeStruct(raw.shape, bf16),
            jax.ShapeDtypeStruct(wk.shape, bf16),
            jax.ShapeDtypeStruct(rk.shape, bf16),
            jax.ShapeDtypeStruct((3, few), f32),
        ),
        in_specs=[hbm, vmem, vmem, vmem, hbm, vmem, vmem, vmem],
        out_specs=(hbm, vmem, vmem, vmem, vmem),
        scratch_shapes=list(space.values()),
        compiler_params=pltpu.CompilerParams(
            vmem_limit_bytes=60 * 1024 * 1024, collective_id=1, has_side_effects=True
        ),
    )(x, raw, wk, rk, g, decay.reshape(1, few), skip.reshape(1, few), bias.reshape(1, few))


def settle(*refs):
    half = len(refs) // 2
    for src, dst in zip(refs[:half], refs[half:]):
        dst[...] = src[...]


def settled(arrays):
    steps = 4
    wide = arrays[0].shape[1] // steps
    blocks = [pl.BlockSpec((arrays[0].shape[0], wide), lambda i: (0, i))]
    blocks += [pl.BlockSpec(a.shape, lambda i: (0, 0)) for a in arrays[1:]]
    return pl.pallas_call(
        settle,
        grid=(steps,),
        out_shape=tuple(jax.ShapeDtypeStruct(a.shape, a.dtype) for a in arrays),
        in_specs=blocks,
        out_specs=tuple(blocks),
        compiler_params=pltpu.CompilerParams(vmem_limit_bytes=60 * 1024 * 1024),
    )(*arrays)


def shards(n, replicas, inputs, raw_step, write_keys, read_keys, grad_out, decay_log, skip_gain, step_bias):
    whole = chip_backward if n == 4 else backward
    dx, step, dwrite, dread, par = settled(whole(
        n, replicas, inputs[0], raw_step[0].T, write_keys[0], read_keys[0], grad_out[0],
        decay_log, skip_gain, step_bias,
    ))
    return dx[None], step.T[None], dwrite[None], dread[None], par


def solution(mesh):
    rows = P("dp", "seq", None)
    return jax.shard_map(
        functools.partial(shards, mesh.shape["seq"], mesh.shape["dp"]),
        mesh=mesh,
        in_specs=(rows,) * 5 + (P("seq"),) * 3,
        out_specs=(rows,) * 4 + (P(None, "seq"),),
        check_vma=False,
    )
```

time: 64.7 us -> 51.1 us (0.79)
  local copies, waits for them, and re-layouts: 7.18 us -> 0 us
  Pallas kernels: 56.5 us -> 50.2 us
    unnamed x12 -> x0, local copies, waits for them, and re-layouts: 7.18 us -> none
    pallas_call x1 -> x2, Pallas kernels: 56.5 us -> 50.2 us  [the longest x1 46.8 us: chip_backward(): pl.pallas_call(functools.partial(chip_kernel, tuple(space), n, replicas),...]
where the time goes in v2:
time: 51.1 us; the launch traced here: 50.8 us
  Pallas kernels  50.2 us (98%)
  between operations  0.64 us (1%)
    pallas_call x1, Pallas kernels, chip_backward(): pl.pallas_call(functools.partial(chip_kernel, tuple(space), n, replicas),...  46.8 us
    pallas_call x1, Pallas kernels, settled(): pl.pallas_call(settle, grid=(steps,), out_shape=tuple((jax.ShapeDtypeStru...  3.42 us

profile of v2, /device:TPU:0, one launch (start us, length us, event | category | flops | bytes accessed | tf_op | source)
XLA Modules:
  0.0 50.8 jit_solution(18169686974770598518)
XLA Ops:
  0.6 46.8 %shard_map.119 = (bf16[128,4096]{1,0:T(8,128)(2,1)}, bf16[64,128]{1,0:T(8,128)(2,1)}, bf16[128,128]{1,0:T(8,128)(2,1)}, bf16[128,128]{1,0:T(8,128)(2,1)}, f32[3,16]{1,0:T(4,128)}) custom-call(bf16[128,4096]{1,0:T(8,128)(2,1)} %bitcast.16, bf16[64,128]{1,0:T(8,128)(2,1)} %bitcast.20, bf16[128,128]{1,0:T(8,128)(2,1)} %bitcast.18, bf16[128,128]{1,0:T(8,128)(2,1)} %bitcast.19, ...), custom_call_target="tpu_custom_call" | custom-call | tf_op jit(solution)/shard_map/pallas_call | solution.py:760
  47.4 3.4 %shard_map.120 = (bf16[128,4096]{1,0:T(8,128)(2,1)}, bf16[64,128]{1,0:T(8,128)(2,1)}, bf16[128,128]{1,0:T(8,128)(2,1)}, bf16[128,128]{1,0:T(8,128)(2,1)}, f32[3,16]{1,0:T(4,128)}) custom-call(bf16[128,4096]{1,0:T(8,128)(2,1)} %get-tuple-element.15.refs_0_, bf16[64,128]{1,0:T(8,128)(2,1)} %get-tuple-element.16.refs_1_, ...), custom_call_target="tpu_custom_call" | custom-call | tf_op jit(solution)/shard_map/pallas_call | solution.py:789

commit v3 on v2

--- a/solution.py
+++ b/solution.py
@@ -493,11 +493,14 @@
     heads = 2 * few
     pairs = heads // 2
     span = pairs * LANES
+    group = 4 if pairs % 4 == 0 else 1
+    broad = group * LANES
+    groups = pairs // group
     me, dp = lax.axis_index("seq"), lax.axis_index("dp")
     chip, core = me // 2, lax.rem(me, 2)
     first = chip == 0
     near, far = me + 1 - 2 * core, lax.rem(me + 2, n)
-    x, g, bk, ck, raws = (scr.x, scr.g, scr.bk, scr.ck, scr.raws)
+    x, g, bk, ck, raws = (scr.both.at[0], scr.both.at[1], scr.bk, scr.ck, scr.raws)
     dxf, dx = scr.dxf, scr.dx
     mine = pl.ds(pl.multiple_of(core * rows, rows), rows)
     theirs = pl.ds(pl.multiple_of((1 - core) * rows, rows), rows)
@@ -547,8 +550,8 @@
     ]
 
     def entry_copies(p):
-        there = pl.ds(pl.multiple_of(near % 2 * span + p * LANES, LANES), LANES)
-        here = pl.ds(pl.multiple_of(p * LANES, LANES), LANES)
+        there = pl.ds(pl.multiple_of((1 - core) * span + p * broad, LANES), broad)
+        here = pl.ds(pl.multiple_of(p * broad, LANES), broad)
         return [
             send(x_hbm.at[:, there], x.at[mine, here], "gox", p, {"seq": near}),
             send(g_hbm.at[:, there], g.at[mine, here], "gog", p, {"seq": near}),
@@ -558,8 +561,8 @@
         return send(scr.state.at[p], scr.state_got.at[p], "state", p, {"seq": far})
 
     def exit_copy(p):
-        here = pl.ds(pl.multiple_of(p * LANES, LANES), LANES)
-        there = pl.ds(pl.multiple_of(core * span + p * LANES, LANES), LANES)
+        here = pl.ds(pl.multiple_of(p * broad, LANES), broad)
+        there = pl.ds(pl.multiple_of(core * span + p * broad, LANES), broad)
         return send(dx.at[theirs, here], dx_out.at[:, there], "back", p, {"seq": near})
 
     for k in range(1, n):
@@ -572,7 +575,7 @@
             copy.start()
         return 0
 
-    lax.fori_loop(0, pairs, launch, 0)
+    lax.fori_loop(0, groups, launch, 0)
     for k in range(1, n):
         prm_copy(k).wait_recv()
     for copy in key_copies:
@@ -592,33 +595,31 @@
     tail = a[:, length - 1 :] - a + jnp.log(scr.dts[...]) * LOG2E
     reach = jnp.exp2(jnp.where(first, tail, a))
     reach = jnp.concatenate([reach, jnp.zeros((LANES - heads, length), f32)], axis=0).T
-    for h in range(heads):
-        scr.reach[h] = jnp.broadcast_to(reach[:, h : h + 1], (length, LANES))
+    low = iota((length, LANES), 1) < LANES // 2
+    for p in range(pairs):
+        one, two = reach[:, 2 * p : 2 * p + 1], reach[:, 2 * p + 1 : 2 * p + 2]
+        spot = p % group * LANES
+        scr.reach[p // group, :, spot : spot + LANES] = jnp.where(low, one, two)
     key = jnp.where(first, bk[...].astype(f32), ck[...].astype(f32))
     scr.key[...] = key.astype(bf16)
     scr.keyt[...] = key.T.astype(bf16)
     for copy in own:
         copy.wait()
-    low = iota((length, LANES), 1) < LANES // 2
     low_row = iota((1, LANES), 1) < LANES // 2
 
-    def weigh(p):
-        here = pl.ds(pl.multiple_of(p * LANES, LANES), LANES)
-        reach = jnp.where(low, scr.reach[2 * p], scr.reach[2 * p + 1])
-        value = jnp.where(first, x[:, here].astype(f32), g[:, here].astype(f32))
-        return here, reach, value
-
-    def states(p, _):
-        for copy in entry_copies(p):
+    def states(q, _):
+        for copy in entry_copies(q):
             copy.wait_recv()
-        _, reach, value = weigh(p)
-        hi, lo = split_two(reach * value)
+        here = pl.ds(pl.multiple_of(q * broad, LANES), broad)
+        hi, lo = split_two(scr.reach[q] * scr.both[chip, :, here].astype(f32))
+        scr.high[q] = hi
+        scr.rest[q] = lo
         kt = scr.keyt[...]
-        scr.state[p] = dot_nn(kt, hi) + dot_nn(kt, lo)
-        state_copy(p).start()
+        scr.state[q] = dot_nn(kt, hi) + dot_nn(kt, lo)
+        state_copy(q).start()
         return 0
 
-    lax.fori_loop(0, pairs, states, 0)
+    lax.fori_loop(0, groups, states, 0)
     scores(bk, ck, scr, length)
     scr.col[...] = jnp.zeros_like(scr.col)
 
@@ -637,25 +638,24 @@
     key_grads(bk, ck, scr, length, write)
     scr.kcross[...] = jnp.zeros_like(scr.kcross)
     scr.zcross[...] = jnp.zeros_like(scr.zcross)
-    lane = iota((length, LANES), 1)
-
-    def across(p, _):
-        state_copy(p).wait_recv()
-        here, reach, value = weigh(p)
-        shi, slo = split_two(scr.state_got[p])
+
+    def across(q, _):
+        state_copy(q).wait_recv()
+        here = pl.ds(pl.multiple_of(q * broad, LANES), broad)
+        shi, slo = split_two(scr.state_got[q])
         k = scr.key[...]
-        u = reach * (dot_nn(k, shi) + dot_nn(k, slo))
-        whi, wlo = split_two(reach * value)
+        whi, wlo = scr.high[q], scr.rest[q]
+        u = scr.reach[q] * (dot_nn(k, shi) + dot_nn(k, slo))
         scr.kcross[...] += dot_nt(whi, shi) + (dot_nt(whi, slo) + dot_nt(wlo, shi))
-        both = value * u
-        one = jnp.sum(jnp.where(low, both, 0.0), axis=1, keepdims=True)
-        two = jnp.sum(jnp.where(low, 0.0, both), axis=1, keepdims=True)
-        scr.zcross[...] += jnp.where(lane == 2 * p, one, 0.0) + jnp.where(lane == 2 * p + 1, two, 0.0)
+        hi, lo = split_two(scr.both[chip, :, here].astype(f32) * u)
+        head = 2 * group * q + iota((broad, LANES), 0) // (LANES // 2)
+        pick = jnp.where(iota((broad, LANES), 1) == head, 1.0, 0.0).astype(bf16)
+        scr.zcross[...] += dot_nn(hi, pick) + dot_nn(lo, pick)
         dx[:, here] = (dxf[:, here] + jnp.where(first, u, 0.0)).astype(bf16)
-        exit_copy(p).start()
+        exit_copy(q).start()
         return 0
 
-    lax.fori_loop(0, pairs, across, 0)
+    lax.fori_loop(0, groups, across, 0)
     keep = pltpu.make_async_copy(dx.at[mine, :], dx_out.at[:, left], scr.own.at[2])
     keep.start()
     kcross = scr.kcross[...]
@@ -706,7 +706,7 @@
         exit_copy(p).wait()
         return 0
 
-    lax.fori_loop(0, pairs, drain, 0)
+    lax.fori_loop(0, groups, drain, 0)
     for copy in key_copies + [sum_copy, step_copy]:
         copy.wait_send()
     for k in range(1, n):
@@ -721,9 +721,12 @@
     few = decay.shape[0]
     heads, length = 2 * few, 2 * rows
     pairs = heads // 2
+    group = 4 if pairs % 4 == 0 else 1
+    groups, broad = pairs // group, group * LANES
     space = scratch(heads, length) | dict(
-        x=pltpu.VMEM((length, pairs * LANES), bf16),
-        g=pltpu.VMEM((length, pairs * LANES), bf16),
+        both=pltpu.VMEM((2, length, pairs * LANES), bf16),
+        high=pltpu.VMEM((groups, length, broad), bf16),
+        rest=pltpu.VMEM((groups, length, broad), bf16),
         dx=pltpu.VMEM((length, pairs * LANES), bf16),
         dxf=pltpu.VMEM((length, pairs * LANES), f32),
         bk=pltpu.VMEM((length, LANES), bf16),
@@ -731,10 +734,10 @@
         key=pltpu.VMEM((length, LANES), bf16),
         keyt=pltpu.VMEM((LANES, length), bf16),
         raws=pltpu.VMEM((length // rows, total, rows), bf16),
-        reach=pltpu.VMEM((heads, length, LANES), f32),
+        reach=pltpu.VMEM((groups, length, broad), f32),
         skips=pltpu.VMEM((heads, 8, LANES), f32),
-        state=pltpu.VMEM((pairs, LANES, LANES), f32),
-        state_got=pltpu.VMEM((pairs, LANES, LANES), f32),
+        state=pltpu.VMEM((groups, LANES, broad), f32),
+        state_got=pltpu.VMEM((groups, LANES, broad), f32),
         kcross=pltpu.VMEM((length, LANES), f32),
         zcross=pltpu.VMEM((length, LANES), f32),
         dkeys=pltpu.VMEM((length, 2 * LANES), f32),
@@ -750,7 +753,7 @@
         own=pltpu.SemaphoreType.DMA((3,)),
     )
     counts = dict(
-        prm=n, key=3, gox=pairs, gog=pairs, state=pairs, back=pairs, dk=1, st=1, par=replicas, tot=n
+        prm=n, key=3, gox=groups, gog=groups, state=groups, back=groups, dk=1, st=1, par=replicas, tot=n
     )
     for name, count in counts.items():
         space[name + "_out"] = pltpu.SemaphoreType.DMA((count,))
@@ -776,22 +779,33 @@
 
 
 def settle(*refs):
-    half = len(refs) // 2
-    for src, dst in zip(refs[:half], refs[half:]):
+    half = (len(refs) - 1) // 2
+    sems = refs[-1]
+    cuts = sems.shape[0]
+    rows = refs[0].shape[0] // cuts
+    copies = [
+        pltpu.make_async_copy(
+            refs[0].at[pl.ds(k * rows, rows), :], refs[half].at[pl.ds(k * rows, rows), :], sems.at[k]
+        )
+        for k in range(cuts)
+    ]
+    for copy in copies:
+        copy.start()
+    for src, dst in zip(refs[1:half], refs[half + 1 : -1]):
         dst[...] = src[...]
+    for copy in copies:
+        copy.wait()
 
 
 def settled(arrays):
-    steps = 4
-    wide = arrays[0].shape[1] // steps
-    blocks = [pl.BlockSpec((arrays[0].shape[0], wide), lambda i: (0, i))]
-    blocks += [pl.BlockSpec(a.shape, lambda i: (0, 0)) for a in arrays[1:]]
+    hbm, vmem = pl.BlockSpec(memory_space=pl.ANY), pl.BlockSpec(memory_space=pltpu.VMEM)
+    blocks = [hbm] + [vmem] * (len(arrays) - 1)
     return pl.pallas_call(
         settle,
-        grid=(steps,),
         out_shape=tuple(jax.ShapeDtypeStruct(a.shape, a.dtype) for a in arrays),
         in_specs=blocks,
         out_specs=tuple(blocks),
+        scratch_shapes=[pltpu.SemaphoreType.DMA((8,))],
         compiler_params=pltpu.CompilerParams(vmem_limit_bytes=60 * 1024 * 1024),
     )(*arrays)
 

time: 51.1 us -> 81.5 us (1.59)
  Pallas kernels: 50.2 us -> 80.6 us
    pallas_call x1, Pallas kernels: 3.42 us -> 34.4 us  [settled(): pl.pallas_call(settle, out_shape=tuple((jax.ShapeDtypeStruct(a.shape, a.d...]
where the time goes in v3:
time: 81.5 us; the launch traced here: 81.2 us
  Pallas kernels  80.6 us (99%)
    pallas_call x1, Pallas kernels, chip_backward(): pl.pallas_call(functools.partial(chip_kernel, tuple(space), n, replicas),...  46.2 us
    pallas_call x1, Pallas kernels, settled(): pl.pallas_call(settle, out_shape=tuple((jax.ShapeDtypeStruct(a.shape, a.d...  34.4 us

profile of v3, /device:TPU:0, one launch (start us, length us, event | category | flops | bytes accessed | tf_op | source)
XLA Modules:
  0.0 81.2 jit_solution(7146262011244028742)
XLA Ops:
  0.6 46.2 %shard_map.119 = (bf16[128,4096]{1,0:T(8,128)(2,1)}, bf16[64,128]{1,0:T(8,128)(2,1)}, bf16[128,128]{1,0:T(8,128)(2,1)}, bf16[128,128]{1,0:T(8,128)(2,1)}, f32[3,16]{1,0:T(4,128)}) custom-call(bf16[128,4096]{1,0:T(8,128)(2,1)} %bitcast.16, bf16[64,128]{1,0:T(8,128)(2,1)} %bitcast.20, bf16[128,128]{1,0:T(8,128)(2,1)} %bitcast.18, bf16[128,128]{1,0:T(8,128)(2,1)} %bitcast.19, ...), custom_call_target="tpu_custom_call" | custom-call | tf_op jit(solution)/shard_map/pallas_call | solution.py:763
  46.9 34.4 %shard_map.120 = (bf16[128,4096]{1,0:T(8,128)(2,1)}, bf16[64,128]{1,0:T(8,128)(2,1)}, bf16[128,128]{1,0:T(8,128)(2,1)}, bf16[128,128]{1,0:T(8,128)(2,1)}, f32[3,16]{1,0:T(4,128)}) custom-call(bf16[128,4096]{1,0:T(8,128)(2,1)} %get-tuple-element.15.refs_0_, bf16[64,128]{1,0:T(8,128)(2,1)} %get-tuple-element.16.refs_1_, ...), custom_call_target="tpu_custom_call" | custom-call | tf_op jit(solution)/shard_map/pallas_call | solution.py:803

commit v4 on v3

--- a/solution.py
+++ b/solution.py
@@ -779,21 +779,21 @@
 
 
 def settle(*refs):
-    half = (len(refs) - 1) // 2
-    sems = refs[-1]
-    cuts = sems.shape[0]
+    half = (len(refs) - 3) // 2
+    held, arrive, leave = refs[-3:]
+    cuts = arrive.shape[0]
     rows = refs[0].shape[0] // cuts
-    copies = [
-        pltpu.make_async_copy(
-            refs[0].at[pl.ds(k * rows, rows), :], refs[half].at[pl.ds(k * rows, rows), :], sems.at[k]
-        )
-        for k in range(cuts)
-    ]
-    for copy in copies:
+    spots = [pl.ds(k * rows, rows) for k in range(cuts)]
+    ins = [pltpu.make_async_copy(refs[0].at[s, :], held.at[s, :], arrive.at[k]) for k, s in enumerate(spots)]
+    outs = [pltpu.make_async_copy(held.at[s, :], refs[half].at[s, :], leave.at[k]) for k, s in enumerate(spots)]
+    for copy in ins:
         copy.start()
-    for src, dst in zip(refs[1:half], refs[half + 1 : -1]):
+    for src, dst in zip(refs[1:half], refs[half + 1 : -3]):
         dst[...] = src[...]
-    for copy in copies:
+    for one, two in zip(ins, outs):
+        one.wait()
+        two.start()
+    for copy in outs:
         copy.wait()
 
 
@@ -805,7 +805,11 @@
         out_shape=tuple(jax.ShapeDtypeStruct(a.shape, a.dtype) for a in arrays),
         in_specs=blocks,
         out_specs=tuple(blocks),
-        scratch_shapes=[pltpu.SemaphoreType.DMA((8,))],
+        scratch_shapes=[
+            pltpu.VMEM(arrays[0].shape, bf16),
+            pltpu.SemaphoreType.DMA((4,)),
+            pltpu.SemaphoreType.DMA((4,)),
+        ],
         compiler_params=pltpu.CompilerParams(vmem_limit_bytes=60 * 1024 * 1024),
     )(*arrays)
 

time: 81.5 us -> 50.6 us (0.62)
  Pallas kernels: 80.6 us -> 49.6 us
    pallas_call x1, Pallas kernels: 34.4 us -> 3.41 us  [settled(): pl.pallas_call(settle, out_shape=tuple((jax.ShapeDtypeStruct(a.shape, a.d...]
where the time goes in v4:
time: 50.6 us; the launch traced here: 50.3 us
  Pallas kernels  49.6 us (98%)
  between operations  0.64 us (1%)
    pallas_call x1, Pallas kernels, chip_backward(): pl.pallas_call(functools.partial(chip_kernel, tuple(space), n, replicas),...  46.2 us
    pallas_call x1, Pallas kernels, settled(): pl.pallas_call(settle, out_shape=tuple((jax.ShapeDtypeStruct(a.shape, a.d...  3.41 us

profile of v4, /device:TPU:0, one launch (start us, length us, event | category | flops | bytes accessed | tf_op | source)
XLA Modules:
  0.0 50.3 jit_solution(13663109382287467609)
XLA Ops:
  0.6 46.2 %shard_map.119 = (bf16[128,4096]{1,0:T(8,128)(2,1)}, bf16[64,128]{1,0:T(8,128)(2,1)}, bf16[128,128]{1,0:T(8,128)(2,1)}, bf16[128,128]{1,0:T(8,128)(2,1)}, f32[3,16]{1,0:T(4,128)}) custom-call(bf16[128,4096]{1,0:T(8,128)(2,1)} %bitcast.16, bf16[64,128]{1,0:T(8,128)(2,1)} %bitcast.20, bf16[128,128]{1,0:T(8,128)(2,1)} %bitcast.18, bf16[128,128]{1,0:T(8,128)(2,1)} %bitcast.19, ...), custom_call_target="tpu_custom_call" | custom-call | tf_op jit(solution)/shard_map/pallas_call | solution.py:763
  46.9 3.4 %shard_map.120 = (bf16[128,4096]{1,0:T(8,128)(2,1)}, bf16[64,128]{1,0:T(8,128)(2,1)}, bf16[128,128]{1,0:T(8,128)(2,1)}, bf16[128,128]{1,0:T(8,128)(2,1)}, f32[3,16]{1,0:T(4,128)}) custom-call(bf16[128,4096]{1,0:T(8,128)(2,1)} %get-tuple-element.15.refs_0_, bf16[64,128]{1,0:T(8,128)(2,1)} %get-tuple-element.16.refs_1_, ...), custom_call_target="tpu_custom_call" | custom-call | tf_op jit(solution)/shard_map/pallas_call | solution.py:803
